TPU v7x, 256 devices: a whole 4x4x8 slice. The times are simulated.
256 devices in a mesh: seq: 128 (over x, z, y_hi, core), head: 2 (over y_lo).
Axes of the slice: x: 4, y: 4 (y_hi: 2, y_lo: 2; y = y_hi * 2 + y_lo), z: 8, core: 2. Of those that a mesh axis runs over, the one named last changes fastest.
Arguments:
- queries: bfloat16 [65536, 512], P('seq', 'head'), may hold values from -60 to 60
- key_vectors: bfloat16 [65536, 512], P('seq', 'head'), may hold values from -6 to 6
- value_vectors: bfloat16 [65536, 512], P('seq', 'head'), may hold values from -6 to 6
- out_grad: bfloat16 [65536, 512], P('seq', 'head'), may hold values from -6 to 6
- out_weight: bfloat16 [512, 512], P('head'), may hold values from -0.25 to 0.25
- mid_keep: int32 [256, 48], P('seq'), may hold values 0 or 1
- frame_keep: int32 [256], P('seq'), may hold values from 0 to 1, as said below
Outputs:
- output: bfloat16 [65536, 512], P('seq', 'head')
- query_gradient: bfloat16 [65536, 512], P('seq', 'head')
- key_gradient: bfloat16 [65536, 512], P('seq', 'head')
- value_gradient: bfloat16 [65536, 512], P('seq', 'head')
- weight_grad: float32 [512, 512], P('head')
Inputs may be any that keep to these rules, and one draw needn't show every extreme that they name: `frame_keep`: frame boundaries fall only inside shards: the first near block of every shard of 512 tokens holds 1.
All inputs are finite; a program needn't handle non-finite values. No bound on the sum of `mid_keep` on one device may be relied on, other than what follows from the above.
Results may differ from a plain program's by a relative error of at most 0.0057.
The roundings to bfloat16 on the way count: a program that leaves them out, or rounds other values in their place, can miss the bound.
Values may be sent and summed in bfloat16 or wider, within the bound.
A program may use at most 64 MiB of HBM per device.

v0:
```python
import math

import jax
import jax.numpy as jnp
from jax import lax
from jax.sharding import Mesh
from jax.sharding import PartitionSpec as P

HDIM = 64
NEAR = 256
MIDG = 8
FARG = 128
REACH = 12
SEQ = ("seq_0", "seq_1", "seq_2", "seq_3")


def laid_out(parts, dim):
    parts = jnp.moveaxis(parts, 0, dim)
    shape = parts.shape
    return parts.reshape(*shape[:dim], shape[dim] * shape[dim + 1], *shape[dim + 2 :])


def sent_to_all(array, axis):
    copies = jnp.broadcast_to(array, (lax.axis_size(axis), *array.shape))
    return lax.all_to_all(copies, axis, split_axis=0, concat_axis=0, tiled=True)


def gathered_copies(array, axis, dim):
    return laid_out(sent_to_all(array, axis), dim)


def shifted(block, axis, distance):
    devices = range(lax.axis_size(axis))
    route = [(i - distance, i) for i in devices if i - distance in devices]
    return lax.ppermute(block, axis, route)


def side_by_side(arrays, axis, dim, along):
    widths = [a.shape[along] for a in arrays]
    both = jnp.concatenate(arrays, axis=along)
    out = lax.all_gather(both, axis, axis=dim, tiled=True)
    return tuple(jnp.split(out, [sum(widths[:k]) for k in range(1, len(widths))], axis=along))


def cut_along(array, dim, peers):
    before, after = (array.shape[:dim], array.shape[dim + 1 :])
    return jnp.moveaxis(array.reshape(*before, peers, -1, *after), dim, 0)


def summed_on_arrival(array, axis, dim):
    peers = lax.axis_size(axis)
    parts = lax.all_to_all(cut_along(array, dim, peers), axis, 0, 0, tiled=True)
    return jnp.sum(parts, axis=0)


def sum_by_axis(array, axes, dim):
    far, near = axes
    own = summed_on_arrival(cut_along(array, dim, lax.axis_size(far)), near, dim + 1)
    return jnp.sum(lax.all_to_all(own, far, 0, 0, tiled=True), axis=0)


def sent_together(arrays, axis, dim, along):
    both = jnp.concatenate(arrays, axis=along)
    out, at, done = (sum_by_axis(both, axis, dim), 0, [])
    for a in arrays:
        done.append(lax.slice_in_dim(out, at, at + a.shape[along], axis=along))
        at += a.shape[along]
    return tuple(done)


def filled_up(lines, peers):
    spare = -lines.shape[0] % peers
    if not spare:
        return lines
    return jnp.concatenate([lines, jnp.zeros((spare, *lines.shape[1:]), lines.dtype)])


def whole_of(array, axes, dim):
    far, near = axes
    parts = sent_to_all(sent_to_all(array, far), near)
    return laid_out(parts.swapaxes(0, 1).reshape(-1, *array.shape), dim)


def nested_sum(array, axes):
    lines = array.reshape(-1)
    padded = filled_up(lines, lax.axis_size(axes[0]) * lax.axis_size(axes[1]))
    whole = whole_of(sum_by_axis(padded, axes, 0), axes, 0)
    return lax.slice_in_dim(whole, 0, len(lines)).reshape(array.shape)


def pooled(source, stride, rooted):
    total = source.astype(jnp.float32).reshape(-1, stride, source.shape[1]).sum(axis=1)
    divisor = math.sqrt(stride) if rooted else float(stride)
    return (total / divisor).astype(jnp.bfloat16)


def visibility(block_id, device_id, length, frame_flag, keep_row, coarse_count):
    query_pos = block_id * NEAR + jnp.arange(NEAR, dtype=jnp.int32)[:, None]
    near_pos = (block_id - 1) * NEAR + jnp.arange(2 * NEAR, dtype=jnp.int32)[None, :]
    near_seen = (
        (near_pos <= query_pos)
        & (near_pos >= 0)
        & ((near_pos >= block_id * NEAR) | (frame_flag == 1))
    )
    groups = length // MIDG
    starts = ((device_id - REACH) * groups + jnp.arange(REACH * groups, dtype=jnp.int32)) * MIDG
    kept = jnp.repeat(keep_row, FARG // MIDG) == 1
    middle_seen = (starts >= 0) & (starts + MIDG <= (block_id - 1) * NEAR) & kept
    far_seen = (jnp.arange(coarse_count, dtype=jnp.int32) + 1) * FARG <= (block_id - 1) * NEAR
    columns = jnp.concatenate([middle_seen, far_seen])
    return jnp.concatenate(
        [near_seen, jnp.broadcast_to(columns[None, :], (NEAR, columns.shape[0]))], axis=1
    )


def attend(query_tile, key_tile, value_tile, visible, gradient_tile, scale_amount):
    logit_matrix = (
        jnp.einsum("aos,ros->oar", query_tile, key_tile, preferred_element_type=jnp.float32)
        * scale_amount
    )
    logit_matrix = jnp.where(visible[None], logit_matrix, -1e30)
    row_top = jnp.max(logit_matrix, axis=2, keepdims=True)
    weights = jnp.exp(logit_matrix - row_top)
    shares = weights / jnp.sum(weights, axis=2, keepdims=True)
    rounded_scores = shares.astype(jnp.bfloat16)
    mixed_result = jnp.einsum(
        "svu,usc->vsc", rounded_scores, value_tile, preferred_element_type=jnp.float32
    ).astype(jnp.bfloat16)
    shared_gradient = jnp.einsum(
        "aos,ros->oar", gradient_tile, value_tile, preferred_element_type=jnp.float32
    )
    centre = jnp.sum(shares * shared_gradient, axis=2, keepdims=True)
    decay_slopes = (shares * (shared_gradient - centre)).astype(jnp.bfloat16)
    query_gradient = (
        jnp.einsum("svu,usc->vsc", decay_slopes, key_tile, preferred_element_type=jnp.float32)
        * scale_amount
    )
    key_gradient = (
        jnp.einsum("equ,qeb->ueb", decay_slopes, query_tile, preferred_element_type=jnp.float32)
        * scale_amount
    )
    value_gradient = jnp.einsum(
        "equ,qeb->ueb", rounded_scores, gradient_tile, preferred_element_type=jnp.float32
    )
    return (mixed_result, query_gradient, key_gradient, value_gradient)


def portion(source, distance, groups):
    start_row = (REACH - distance) * groups
    return source[start_row : start_row + groups]


def joined(stacked):
    return jnp.moveaxis(stacked, 0, 1).reshape(stacked.shape[1], -1)


def on_device(queries, key_vectors, value_vectors, out_grad, out_weight, mid_keep, frame_keep):
    length, feature_count = queries.shape
    blocks = length // NEAR
    groups = length // MIDG
    window_rows = REACH * groups
    pair_count = feature_count // (2 * HDIM)
    scale_amount = HDIM ** (-0.5)
    seq_index = lax.axis_index(SEQ)
    whole_grad = gathered_copies(out_grad, "head", 1)
    mixed_grad = lax.dot_general(
        whole_grad, out_weight, (((1,), (1,)), ((), ())), preferred_element_type=jnp.float32
    ).astype(jnp.bfloat16)
    rim_keys, rim_values = shifted(
        (key_vectors[length - NEAR :], value_vectors[length - NEAR :]), SEQ, 1
    )
    near_keys = jnp.concatenate([rim_keys, key_vectors], axis=0)
    near_values = jnp.concatenate([rim_values, value_vectors], axis=0)
    middle_keys = pooled(key_vectors, MIDG, True)
    middle_values = pooled(value_vectors, MIDG, False)
    pieces = []
    for distance in range(REACH, 0, -1):
        pieces.append(shifted((middle_keys, middle_values), SEQ, distance))
    window_keys = jnp.concatenate([piece[0] for piece in pieces], axis=0)
    window_values = jnp.concatenate([piece[1] for piece in pieces], axis=0)
    coarse_keys, coarse_values = side_by_side(
        (pooled(key_vectors, FARG, True), pooled(value_vectors, FARG, False)), SEQ, 0, 1
    )
    coarse_count = coarse_keys.shape[0]
    block_views = [
        visibility(
            seq_index * blocks + block_at,
            seq_index,
            length,
            frame_keep[block_at],
            mid_keep[block_at],
            coarse_count,
        )
        for block_at in range(blocks)
    ]

    def pair_pass(pair_index):
        offset = pair_index * 2 * HDIM

        def columns(source):
            return lax.dynamic_slice_in_dim(source, offset, 2 * HDIM, 1).reshape(
                source.shape[0], 2, HDIM
            )

        query_heads = columns(queries)
        grad_heads = columns(mixed_grad)
        near_kh = columns(near_keys)
        near_vh = columns(near_values)
        window_kh = columns(window_keys)
        window_vh = columns(window_values)
        coarse_kh = columns(coarse_keys)
        coarse_vh = columns(coarse_values)
        near_kg = jnp.zeros((NEAR + length, 2, HDIM), jnp.float32)
        near_vg = jnp.zeros((NEAR + length, 2, HDIM), jnp.float32)
        window_kg = jnp.zeros((window_rows, 2, HDIM), jnp.float32)
        window_vg = jnp.zeros((window_rows, 2, HDIM), jnp.float32)
        coarse_kg = jnp.zeros((coarse_count, 2, HDIM), jnp.float32)
        coarse_vg = jnp.zeros((coarse_count, 2, HDIM), jnp.float32)
        blended_parts = []
        query_parts = []
        for block_at in range(blocks):
            first_row = block_at * NEAR
            key_tile = jnp.concatenate(
                [near_kh[first_row : first_row + 2 * NEAR], window_kh, coarse_kh], axis=0
            )
            value_tile = jnp.concatenate(
                [near_vh[first_row : first_row + 2 * NEAR], window_vh, coarse_vh], axis=0
            )
            mixed_result, query_part, key_part, value_part = attend(
                query_heads[first_row : first_row + NEAR],
                key_tile,
                value_tile,
                block_views[block_at],
                grad_heads[first_row : first_row + NEAR],
                scale_amount,
            )
            blended_parts.append(mixed_result)
            query_parts.append(query_part)
            near_kg = near_kg.at[first_row : first_row + 2 * NEAR].add(key_part[: 2 * NEAR])
            near_vg = near_vg.at[first_row : first_row + 2 * NEAR].add(value_part[: 2 * NEAR])
            window_kg = window_kg + key_part[2 * NEAR : 2 * NEAR + window_rows]
            window_vg = window_vg + value_part[2 * NEAR : 2 * NEAR + window_rows]
            coarse_kg = coarse_kg + key_part[2 * NEAR + window_rows :]
            coarse_vg = coarse_vg + value_part[2 * NEAR + window_rows :]
        return (
            jnp.concatenate(blended_parts, axis=0),
            jnp.concatenate(query_parts, axis=0),
            near_kg,
            near_vg,
            window_kg,
            window_vg,
            coarse_kg,
            coarse_vg,
        )

    results = lax.map(pair_pass, jnp.arange(pair_count, dtype=jnp.int32))
    attention, query_gradient, near_kg, near_vg, window_kg, window_vg, coarse_kg, coarse_vg = [
        joined(stacked) for stacked in results
    ]
    partial_out = jnp.dot(attention, out_weight, preferred_element_type=jnp.float32)
    output = summed_on_arrival(partial_out, "head", 1).astype(jnp.bfloat16)
    back_keys, back_values = shifted((near_kg[:NEAR], near_vg[:NEAR]), SEQ, -1)
    own_kg = near_kg[NEAR:].at[length - NEAR :].add(back_keys)
    own_vg = near_vg[NEAR:].at[length - NEAR :].add(back_values)
    middle_kg = jnp.zeros((groups, feature_count), jnp.float32)
    middle_vg = jnp.zeros((groups, feature_count), jnp.float32)
    for distance in range(1, REACH + 1):
        returned = (
            shifted(
                portion(window_kg, distance, groups).astype(jnp.bfloat16), SEQ, -distance
            ).astype(jnp.float32),
            shifted(
                portion(window_vg, distance, groups).astype(jnp.bfloat16), SEQ, -distance
            ).astype(jnp.float32),
        )
        middle_kg = middle_kg + returned[0]
        middle_vg = middle_vg + returned[1]
    coarse_own_kg, coarse_own_vg = sent_together(
        (coarse_kg, coarse_vg), (("seq_0", "seq_1", "seq_2"), "seq_3"), 0, 1
    )
    key_gradient = (
        own_kg
        + jnp.repeat(middle_kg, MIDG, axis=0) / math.sqrt(MIDG)
        + jnp.repeat(coarse_own_kg, FARG, axis=0) / math.sqrt(FARG)
    )
    value_gradient = (
        own_vg
        + jnp.repeat(middle_vg, MIDG, axis=0) / MIDG
        + jnp.repeat(coarse_own_vg, FARG, axis=0) / FARG
    )
    token_total = length * lax.axis_size(SEQ)
    local_weight = lax.dot_general(
        attention, whole_grad, (((0,), (0,)), ((), ())), preferred_element_type=jnp.float32
    ) / math.sqrt(token_total)
    weight_grad = nested_sum(local_weight, (("seq_0", "seq_1", "seq_2"), "seq_3"))
    return (
        output,
        query_gradient.astype(jnp.bfloat16),
        key_gradient.astype(jnp.bfloat16),
        value_gradient.astype(jnp.bfloat16),
        weight_grad,
    )


def solution(mesh):
    split = Mesh(
        mesh.devices.reshape(4, 8, 2, 2, mesh.shape["head"]),
        ("seq_0", "seq_1", "seq_2", "seq_3", "head"),
    )
    return jax.shard_map(
        on_device,
        mesh=split,
        in_specs=(
            P(SEQ, "head"),
            P(SEQ, "head"),
            P(SEQ, "head"),
            P(SEQ, "head"),
            P("head", None),
            P(SEQ, None),
            P(SEQ),
        ),
        out_specs=(P(SEQ, "head"), P(SEQ, "head"), P(SEQ, "head"), P(SEQ, "head"), P("head", None)),
        check_vma=False,
    )
```

profile of v0, /device:TPU:1, one launch (start us, length us, event | category | flops | bytes accessed | tf_op | source)
XLA Modules:
  0.0 642.3 jit_solution(3025139766772427952)
XLA Ops:
  1.8 7.2 %collective-permute-start.1 = (bf16[64,256]{1,0:T(8,128)(2,1)S(1)}, bf16[64,256]{1,0:T(8,128)(2,1)S(1)}, u32[]{:S(2)}, u32[]{:S(2)}) collective-permute-start(bf16[64,256]{1,0:T(8,128)(2,1)S(1)} %multiply_convert_fusion.3), channel_id=1, source_target_pairs={{0,24},{2,26},{4,28},{6,30},{8,32},{10,34},{12,36},{14,38},{16,40}... | collective-permute-start | bytes 98312 | tf_op jit(solution)/shard_map/ppermute | solution.py:35
  9.0 6.5 %collective-permute-start.2 = (bf16[64,256]{1,0:T(8,128)(2,1)S(1)}, bf16[64,256]{1,0:T(8,128)(2,1)S(1)}, u32[]{:S(2)}, u32[]{:S(2)}) collective-permute-start(bf16[64,256]{1,0:T(8,128)(2,1)S(1)} %multiply_convert_fusion.3), channel_id=1, source_target_pairs={{0,22},{2,24},{4,26},{6,28},{8,30},{10,32},{12,34},{14,36},{16,38}... | collective-permute-start | bytes 98312 | tf_op jit(solution)/shard_map/ppermute | solution.py:35
  15.5 3.8 collective-permute-start.3
  19.4 6.2 collective-permute-start.4
  25.6 6.1 collective-permute-start.5
  33.7 3.6 all-to-all-start
  40.5 176.6 %all-gather = bf16[128,4,512]{2,1,0:T(4,128)(2,1)S(1)} all-gather(bf16[1,4,512]{2,1,0:T(4,128)(2,1)S(1)} %maximum_bitcast_fusion.3), channel_id=1, replica_groups=mesh['seq_0'=4,'seq_1'=8,'seq_2'=2,'seq_3'=2,'head'=2] {'seq_0','seq_1',..., dimensions={0}, use_global_device_ids=true | all-gather | bytes 528384 | tf_op jit(solution)/shard_map/all_gather | solution.py:41
  228.1 8.3 %collective-permute-start.7 = (bf16[64,256]{1,0:T(8,128)(2,1)S(1)}, bf16[64,256]{1,0:T(8,128)(2,1)S(1)}, u32[]{:S(2)}, u32[]{:S(2)}) collective-permute-start(bf16[64,256]{1,0:T(8,128)(2,1)S(1)} %multiply_convert_fusion.3), channel_id=1, source_target_pairs={{0,12},{2,14},{4,16},{6,18},{8,20},{10,22},{12,24},{14,26},{16,28}... | collective-permute-start | bytes 98312 | tf_op jit(solution)/shard_map/ppermute | solution.py:35
  236.4 3.6 collective-permute-start.8
  243.1 3.4 collective-permute-start.11
  246.5 4.5 collective-permute-start.12
  255.0 6.5 %collective-permute-start.18 = (bf16[64,256]{1,0:T(8,128)(2,1)S(1)}, bf16[64,256]{1,0:T(8,128)(2,1)S(1)}, u32[]{:S(2)}, u32[]{:S(2)}) collective-permute-start(bf16[64,256]{1,0:T(8,128)(2,1)S(1)} %multiply_convert_fusion.2), channel_id=1, source_target_pairs={{0,16},{2,18},{4,20},{6,22},{8,24},{10,26},{12,28},{14,30},{16,32}... | collective-permute-start | bytes 98312 | tf_op jit(solution)/shard_map/ppermute | solution.py:35
  261.6 2.6 collective-permute-start.19
  264.2 3.4 collective-permute-start.20
  268.2 3.7 collective-permute-start.21
  272.6 2.2 collective-permute-start.22
  277.3 3.4 collective-permute-start.24
  281.3 6.2 collective-permute-start.25
  290.6 8.8 %collective-permute-start.13 = (bf16[256,256]{0,1:T(8,128)(2,1)S(1)}, bf16[256,256]{0,1:T(8,128)(2,1)S(1)}, u32[]{:S(2)}, u32[]{:S(2)}) collective-permute-start(bf16[256,256]{0,1:T(8,128)(2,1)S(1)} %slice.507), channel_id=1, source_target_pairs={{0,2},{2,4},{4,6},{6,8},{8,10},{10,12},{12,14},{14,16},{16,18},{18... | collective-permute-start | bytes 393224 | tf_op jit(solution)/shard_map/ppermute | solution.py:35
  302.8 106.0 %while.32 = (s32[]{:T(128)}, bf16[2,512,2,64]{1,3,2,0:T(8,128)(2,1)}, bf16[2,512,2,64]{1,3,2,0:T(8,128)(2,1)}, f32[2,768,2,64]{1,3,2,0:T(8,128)}, f32[2,768,2,64...) while((s32[]{:T(128)}, ...), condition=%wide.region_11.12_spmd, body=%wide.region_4.11_spmd.sunk | while | flops 1935945216 | bytes 155089024 | solution.py:256
  318.6 4.3 exponential_reduce_fusion.4
  324.1 3.2 multiply_reduce_fusion.4
  329.7 4.3 exponential_reduce_fusion.5
  334.2 3.2 multiply_reduce_fusion.5
  341.0 3.5 fusion.135
  344.5 3.4 fusion.136
  349.6 3.7 convolution_bitcast_fusion.5
  353.3 2.9 convolution_bitcast_fusion.6
  366.3 4.3 exponential_reduce_fusion.4
  371.7 3.2 multiply_reduce_fusion.4
  377.4 4.3 exponential_reduce_fusion.5
  381.8 3.2 multiply_reduce_fusion.5
  388.6 3.5 fusion.135
  392.1 3.4 fusion.136
  397.2 3.7 convolution_bitcast_fusion.5
  400.9 2.9 convolution_bitcast_fusion.6
  416.0 3.8 all_to_all.48
  419.8 4.1 all-to-all-start.2
  425.6 22.1 %all-to-all-start.5 = ((f32[64,1,1024]{2,1,0:T(1,128)}), f32[64,1,1024]{2,1,0:T(1,128)S(1)}, u32[]{:S(2)}, u32[]{:S(2)}) async-start(f32[64,1,1024]{2,1,0:T(1,128)} %all_to_all.35), calls=%async_computation.5 | async-start | bytes 524288 | tf_op jit(solution)/shard_map/all_to_all | solution.py:59
  458.7 2.4 convolution_bitcast_fusion.2
  464.8 3.6 all-to-all-start.1
  480.6 2.6 collective-permute-start.27
  516.3 61.6 %all-to-all-start.3 = ((f32[64,4,512]{2,1,0:T(4,128)}), f32[64,4,512]{2,1,0:T(4,128)}, u32[]{:S(2)}, u32[]{:S(2)}) async-start(f32[64,4,512]{2,1,0:T(4,128)} %reduce_sum.134), calls=%async_computation.3 | async-start | bytes 1048576 | tf_op jit(solution)/shard_map/all_to_all | solution.py:59
  585.1 8.2 %collective-permute-done.44 = bf16[64,256]{1,0:T(8,128)(2,1)S(1)} collective-permute-done((bf16[64,256]{1,0:T(8,128)(2,1)}, bf16[64,256]{1,0:T(8,128)(2,1)S(1)}, u32[]{:S(2)}, u32[]{:S(2)}) %collective-permute-start.44) | collective-permute-done | bytes 32800 | tf_op jit(solution)/shard_map/ppermute | solution.py:35
  600.4 2.5 collective-permute-done.26
  608.6 15.6 %all-to-all-start.6 = ((f32[64,1,1024]{2,1,0:T(1,128)}), f32[64,1,1024]{2,1,0:T(1,128)S(1)}, u32[]{:S(2)}, u32[]{:S(2)}) async-start(f32[64,1,1024]{2,1,0:T(1,128)} %broadcast_in_dim.140), calls=%async_computation.6 | async-start | bytes 524288 | tf_op jit(solution)/shard_map/all_to_all | solution.py:25
  628.4 7.9 %all-to-all-done.6 = f32[64,1,1024]{2,1,0:T(1,128)S(1)} async-done(((f32[64,1,1024]{2,1,0:T(1,128)}), f32[64,1,1024]{2,1,0:T(1,128)S(1)}, u32[]{:S(2)}, u32[]{:S(2)}) %all-to-all-start.6) | async-done | bytes 262176 | tf_op jit(solution)/shard_map/all_to_all | solution.py:25
  636.4 3.8 all_to_all.49
  (466 shorter events, 163.8 us)
Async XLA Ops:
  1.8 222.1 %collective-permute-start.1 = (bf16[64,256]{1,0:T(8,128)(2,1)S(1)}, bf16[64,256]{1,0:T(8,128)(2,1)S(1)}, u32[]{:S(2)}, u32[]{:S(2)}) collective-permute-start(bf16[64,256]{1,0:T(8,128)(2,1)S(1)} %multiply_convert_fusion.3), channel_id=1, source_target_pairs={{0,24},{2,26},{4,28},{6,30},{8,32},{10,34},{12,36},{14,38},{16,40}... | collective-permute-start | bytes 98312 | tf_op jit(solution)/shard_map/ppermute | solution.py:35
  9.0 219.1 %collective-permute-start.2 = (bf16[64,256]{1,0:T(8,128)(2,1)S(1)}, bf16[64,256]{1,0:T(8,128)(2,1)S(1)}, u32[]{:S(2)}, u32[]{:S(2)}) collective-permute-start(bf16[64,256]{1,0:T(8,128)(2,1)S(1)} %multiply_convert_fusion.3), channel_id=1, source_target_pairs={{0,22},{2,24},{4,26},{6,28},{8,30},{10,32},{12,34},{14,36},{16,38}... | collective-permute-start | bytes 98312 | tf_op jit(solution)/shard_map/ppermute | solution.py:35
  15.5 220.8 %collective-permute-start.3 = (bf16[64,256]{1,0:T(8,128)(2,1)S(1)}, bf16[64,256]{1,0:T(8,128)(2,1)S(1)}, u32[]{:S(2)}, u32[]{:S(2)}) collective-permute-start(bf16[64,256]{1,0:T(8,128)(2,1)S(1)} %multiply_convert_fusion.3), channel_id=1, source_target_pairs={{0,20},{2,22},{4,24},{6,26},{8,28},{10,30},{12,32},{14,34},{16,36}... | collective-permute-start | bytes 98312 | tf_op jit(solution)/shard_map/ppermute | solution.py:35
  19.4 220.6 %collective-permute-start.4 = (bf16[64,256]{1,0:T(8,128)(2,1)S(1)}, bf16[64,256]{1,0:T(8,128)(2,1)S(1)}, u32[]{:S(2)}, u32[]{:S(2)}) collective-permute-start(bf16[64,256]{1,0:T(8,128)(2,1)S(1)} %multiply_convert_fusion.3), channel_id=1, source_target_pairs={{0,18},{2,20},{4,22},{6,24},{8,26},{10,28},{12,30},{14,32},{16,34}... | collective-permute-start | bytes 98312 | tf_op jit(solution)/shard_map/ppermute | solution.py:35
  25.6 215.7 %collective-permute-start.5 = (bf16[64,256]{1,0:T(8,128)(2,1)S(1)}, bf16[64,256]{1,0:T(8,128)(2,1)S(1)}, u32[]{:S(2)}, u32[]{:S(2)}) collective-permute-start(bf16[64,256]{1,0:T(8,128)(2,1)S(1)} %multiply_convert_fusion.3), channel_id=1, source_target_pairs={{0,16},{2,18},{4,20},{6,22},{8,24},{10,26},{12,28},{14,30},{16,32}... | collective-permute-start | bytes 98312 | tf_op jit(solution)/shard_map/ppermute | solution.py:35
  33.7 268.3 %all-to-all-start = ((bf16[2,512,256]{1,2,0:T(8,128)(2,1)}), bf16[2,512,256]{1,2,0:T(8,128)(2,1)S(1)}, u32[]{:S(2)}, u32[]{:S(2)}) async-start(bf16[2,512,256]{1,2,0:T(8,128)(2,1)} %broadcast_in_dim.135), calls=%async_computation | async-start | bytes 1048576 | tf_op jit(solution)/shard_map/all_to_all | solution.py:25
  226.2 16.9 %collective-permute-start.6 = (bf16[64,256]{1,0:T(8,128)(2,1)S(1)}, bf16[64,256]{1,0:T(8,128)(2,1)S(1)}, u32[]{:S(2)}, u32[]{:S(2)}) collective-permute-start(bf16[64,256]{1,0:T(8,128)(2,1)S(1)} %multiply_convert_fusion.3), channel_id=1, source_target_pairs={{0,14},{2,16},{4,18},{6,20},{8,22},{10,24},{12,26},{14,28},{16,30}... | collective-permute-start | bytes 98312 | tf_op jit(solution)/shard_map/ppermute | solution.py:35
  228.1 18.4 %collective-permute-start.7 = (bf16[64,256]{1,0:T(8,128)(2,1)S(1)}, bf16[64,256]{1,0:T(8,128)(2,1)S(1)}, u32[]{:S(2)}, u32[]{:S(2)}) collective-permute-start(bf16[64,256]{1,0:T(8,128)(2,1)S(1)} %multiply_convert_fusion.3), channel_id=1, source_target_pairs={{0,12},{2,14},{4,16},{6,18},{8,20},{10,22},{12,24},{14,26},{16,28}... | collective-permute-start | bytes 98312 | tf_op jit(solution)/shard_map/ppermute | solution.py:35
  236.4 14.7 %collective-permute-start.8 = (bf16[64,256]{1,0:T(8,128)(2,1)S(1)}, bf16[64,256]{1,0:T(8,128)(2,1)S(1)}, u32[]{:S(2)}, u32[]{:S(2)}) collective-permute-start(bf16[64,256]{1,0:T(8,128)(2,1)S(1)} %multiply_convert_fusion.3), channel_id=1, source_target_pairs={{0,10},{2,12},{4,14},{6,16},{8,18},{10,20},{12,22},{14,24},{16,26}... | collective-permute-start | bytes 98312 | tf_op jit(solution)/shard_map/ppermute | solution.py:35
  240.0 12.3 %collective-permute-start.9 = (bf16[64,256]{1,0:T(8,128)(2,1)S(1)}, bf16[64,256]{1,0:T(8,128)(2,1)S(1)}, u32[]{:S(2)}, u32[]{:S(2)}) collective-permute-start(bf16[64,256]{1,0:T(8,128)(2,1)S(1)} %multiply_convert_fusion.3), channel_id=1, source_target_pairs={{0,8},{2,10},{4,12},{6,14},{8,16},{10,18},{12,20},{14,22},{16,24},... | collective-permute-start | bytes 98312 | tf_op jit(solution)/shard_map/ppermute | solution.py:35
  241.3 12.3 %collective-permute-start.10 = (bf16[64,256]{1,0:T(8,128)(2,1)S(1)}, bf16[64,256]{1,0:T(8,128)(2,1)S(1)}, u32[]{:S(2)}, u32[]{:S(2)}) collective-permute-start(bf16[64,256]{1,0:T(8,128)(2,1)S(1)} %multiply_convert_fusion.3), channel_id=1, source_target_pairs={{0,6},{2,8},{4,10},{6,12},{8,14},{10,16},{12,18},{14,20},{16,22},{... | collective-permute-start | bytes 98312 | tf_op jit(solution)/shard_map/ppermute | solution.py:35
  246.5 15.0 %collective-permute-start.12 = (bf16[64,256]{1,0:T(8,128)(2,1)S(1)}, bf16[64,256]{1,0:T(8,128)(2,1)S(1)}, u32[]{:S(2)}, u32[]{:S(2)}) collective-permute-start(bf16[64,256]{1,0:T(8,128)(2,1)S(1)} %multiply_convert_fusion.3), channel_id=1, source_target_pairs={{0,2},{2,4},{4,6},{6,8},{8,10},{10,12},{12,14},{14,16},{16,18},{18... | collective-permute-start | bytes 98312 | tf_op jit(solution)/shard_map/ppermute | solution.py:35
  251.1 13.1 %collective-permute-start.15 = (bf16[64,256]{1,0:T(8,128)(2,1)S(1)}, bf16[64,256]{1,0:T(8,128)(2,1)S(1)}, u32[]{:S(2)}, u32[]{:S(2)}) collective-permute-start(bf16[64,256]{1,0:T(8,128)(2,1)S(1)} %multiply_convert_fusion.2), channel_id=1, source_target_pairs={{0,22},{2,24},{4,26},{6,28},{8,30},{10,32},{12,34},{14,36},{16,38}... | collective-permute-start | bytes 98312 | tf_op jit(solution)/shard_map/ppermute | solution.py:35
  252.4 15.8 %collective-permute-start.16 = (bf16[64,256]{1,0:T(8,128)(2,1)S(1)}, bf16[64,256]{1,0:T(8,128)(2,1)S(1)}, u32[]{:S(2)}, u32[]{:S(2)}) collective-permute-start(bf16[64,256]{1,0:T(8,128)(2,1)S(1)} %multiply_convert_fusion.2), channel_id=1, source_target_pairs={{0,20},{2,22},{4,24},{6,26},{8,28},{10,30},{12,32},{14,34},{16,36}... | collective-permute-start | bytes 98312 | tf_op jit(solution)/shard_map/ppermute | solution.py:35
  253.7 18.9 %collective-permute-start.17 = (bf16[64,256]{1,0:T(8,128)(2,1)S(1)}, bf16[64,256]{1,0:T(8,128)(2,1)S(1)}, u32[]{:S(2)}, u32[]{:S(2)}) collective-permute-start(bf16[64,256]{1,0:T(8,128)(2,1)S(1)} %multiply_convert_fusion.2), channel_id=1, source_target_pairs={{0,18},{2,20},{4,22},{6,24},{8,26},{10,28},{12,30},{14,32},{16,34}... | collective-permute-start | bytes 98312 | tf_op jit(solution)/shard_map/ppermute | solution.py:35
  255.0 20.4 %collective-permute-start.18 = (bf16[64,256]{1,0:T(8,128)(2,1)S(1)}, bf16[64,256]{1,0:T(8,128)(2,1)S(1)}, u32[]{:S(2)}, u32[]{:S(2)}) collective-permute-start(bf16[64,256]{1,0:T(8,128)(2,1)S(1)} %multiply_convert_fusion.2), channel_id=1, source_target_pairs={{0,16},{2,18},{4,20},{6,22},{8,24},{10,26},{12,28},{14,30},{16,32}... | collective-permute-start | bytes 98312 | tf_op jit(solution)/shard_map/ppermute | solution.py:35
  261.6 15.7 %collective-permute-start.19 = (bf16[64,256]{1,0:T(8,128)(2,1)S(1)}, bf16[64,256]{1,0:T(8,128)(2,1)S(1)}, u32[]{:S(2)}, u32[]{:S(2)}) collective-permute-start(bf16[64,256]{1,0:T(8,128)(2,1)S(1)} %multiply_convert_fusion.2), channel_id=1, source_target_pairs={{0,14},{2,16},{4,18},{6,20},{8,22},{10,24},{12,26},{14,28},{16,30}... | collective-permute-start | bytes 98312 | tf_op jit(solution)/shard_map/ppermute | solution.py:35
  264.2 17.1 %collective-permute-start.20 = (bf16[64,256]{1,0:T(8,128)(2,1)S(1)}, bf16[64,256]{1,0:T(8,128)(2,1)S(1)}, u32[]{:S(2)}, u32[]{:S(2)}) collective-permute-start(bf16[64,256]{1,0:T(8,128)(2,1)S(1)} %multiply_convert_fusion.2), channel_id=1, source_target_pairs={{0,12},{2,14},{4,16},{6,18},{8,20},{10,22},{12,24},{14,26},{16,28}... | collective-permute-start | bytes 98312 | tf_op jit(solution)/shard_map/ppermute | solution.py:35
  268.2 19.9 %collective-permute-start.21 = (bf16[64,256]{1,0:T(8,128)(2,1)S(1)}, bf16[64,256]{1,0:T(8,128)(2,1)S(1)}, u32[]{:S(2)}, u32[]{:S(2)}) collective-permute-start(bf16[64,256]{1,0:T(8,128)(2,1)S(1)} %multiply_convert_fusion.2), channel_id=1, source_target_pairs={{0,10},{2,12},{4,14},{6,16},{8,18},{10,20},{12,22},{14,24},{16,26}... | collective-permute-start | bytes 98312 | tf_op jit(solution)/shard_map/ppermute | solution.py:35
  272.6 18.0 %collective-permute-start.22 = (bf16[64,256]{1,0:T(8,128)(2,1)S(1)}, bf16[64,256]{1,0:T(8,128)(2,1)S(1)}, u32[]{:S(2)}, u32[]{:S(2)}) collective-permute-start(bf16[64,256]{1,0:T(8,128)(2,1)S(1)} %multiply_convert_fusion.2), channel_id=1, source_target_pairs={{0,8},{2,10},{4,12},{6,14},{8,16},{10,18},{12,20},{14,22},{16,24},... | collective-permute-start | bytes 98312 | tf_op jit(solution)/shard_map/ppermute | solution.py:35
  275.4 24.7 %collective-permute-start.23 = (bf16[64,256]{1,0:T(8,128)(2,1)S(1)}, bf16[64,256]{1,0:T(8,128)(2,1)S(1)}, u32[]{:S(2)}, u32[]{:S(2)}) collective-permute-start(bf16[64,256]{1,0:T(8,128)(2,1)S(1)} %multiply_convert_fusion.2), channel_id=1, source_target_pairs={{0,6},{2,8},{4,10},{6,12},{8,14},{10,16},{12,18},{14,20},{16,22},{... | collective-permute-start | bytes 98312 | tf_op jit(solution)/shard_map/ppermute | solution.py:35
  277.3 23.4 %collective-permute-start.24 = (bf16[64,256]{1,0:T(8,128)(2,1)S(1)}, bf16[64,256]{1,0:T(8,128)(2,1)S(1)}, u32[]{:S(2)}, u32[]{:S(2)}) collective-permute-start(bf16[64,256]{1,0:T(8,128)(2,1)S(1)} %multiply_convert_fusion.2), channel_id=1, source_target_pairs={{0,4},{2,6},{4,8},{6,10},{8,12},{10,14},{12,16},{14,18},{16,20},{1... | collective-permute-start | bytes 98312 | tf_op jit(solution)/shard_map/ppermute | solution.py:35
  281.3 20.0 %collective-permute-start.25 = (bf16[64,256]{1,0:T(8,128)(2,1)S(1)}, bf16[64,256]{1,0:T(8,128)(2,1)S(1)}, u32[]{:S(2)}, u32[]{:S(2)}) collective-permute-start(bf16[64,256]{1,0:T(8,128)(2,1)S(1)} %multiply_convert_fusion.2), channel_id=1, source_target_pairs={{0,2},{2,4},{4,6},{6,8},{8,10},{10,12},{12,14},{14,16},{16,18},{18... | collective-permute-start | bytes 98312 | tf_op jit(solution)/shard_map/ppermute | solution.py:35
  288.1 13.8 %collective-permute-start = (bf16[256,256]{0,1:T(8,128)(2,1)S(1)}, bf16[256,256]{0,1:T(8,128)(2,1)S(1)}, u32[]{:S(2)}, u32[]{:S(2)}) collective-permute-start(bf16[256,256]{0,1:T(8,128)(2,1)S(1)} %slice.506), channel_id=1, source_target_pairs={{0,2},{2,4},{4,6},{6,8},{8,10},{10,12},{12,14},{14,16},{16,18},{18... | collective-permute-start | bytes 393224 | tf_op jit(solution)/shard_map/ppermute | solution.py:35
  425.6 39.2 %all-to-all-start.5 = ((f32[64,1,1024]{2,1,0:T(1,128)}), f32[64,1,1024]{2,1,0:T(1,128)S(1)}, u32[]{:S(2)}, u32[]{:S(2)}) async-start(f32[64,1,1024]{2,1,0:T(1,128)} %all_to_all.35), calls=%async_computation.5 | async-start | bytes 524288 | tf_op jit(solution)/shard_map/all_to_all | solution.py:59
  449.3 19.1 %collective-permute-start.38 = (bf16[64,256]{1,0:T(8,128)(2,1)}, bf16[64,256]{1,0:T(8,128)(2,1)S(1)}, u32[]{:S(2)}, u32[]{:S(2)}) collective-permute-start(bf16[64,256]{1,0:T(8,128)(2,1)} %copy.281), channel_id=1, source_target_pairs={{24,0},{26,2},{28,4},{30,6},{32,8},{34,10},{36,12},{38,14},{40,16}... | collective-permute-start | bytes 98312 | tf_op jit(solution)/shard_map/ppermute | solution.py:35
  451.4 18.3 %collective-permute-start.37 = (bf16[64,256]{1,0:T(8,128)(2,1)}, bf16[64,256]{1,0:T(8,128)(2,1)S(1)}, u32[]{:S(2)}, u32[]{:S(2)}) collective-permute-start(bf16[64,256]{1,0:T(8,128)(2,1)} %copy.280), channel_id=1, source_target_pairs={{22,0},{24,2},{26,4},{28,6},{30,8},{32,10},{34,12},{36,14},{38,16}... | collective-permute-start | bytes 98312 | tf_op jit(solution)/shard_map/ppermute | solution.py:35
  453.4 17.6 %collective-permute-start.36 = (bf16[64,256]{1,0:T(8,128)(2,1)}, bf16[64,256]{1,0:T(8,128)(2,1)}, u32[]{:S(2)}, u32[]{:S(2)}) collective-permute-start(bf16[64,256]{1,0:T(8,128)(2,1)} %copy.279), channel_id=1, source_target_pairs={{20,0},{22,2},{24,4},{26,6},{28,8},{30,10},{32,12},{34,14},{36,16}... | collective-permute-start | bytes 98312 | tf_op jit(solution)/shard_map/ppermute | solution.py:35
  455.4 16.9 %collective-permute-start.35 = (bf16[64,256]{1,0:T(8,128)(2,1)}, bf16[64,256]{1,0:T(8,128)(2,1)}, u32[]{:S(2)}, u32[]{:S(2)}) collective-permute-start(bf16[64,256]{1,0:T(8,128)(2,1)} %copy.278), channel_id=1, source_target_pairs={{18,0},{20,2},{22,4},{24,6},{26,8},{28,10},{30,12},{32,14},{34,16}... | collective-permute-start | bytes 98312 | tf_op jit(solution)/shard_map/ppermute | solution.py:35
  457.4 20.6 %collective-permute-start.34 = (bf16[64,256]{1,0:T(8,128)(2,1)}, bf16[64,256]{1,0:T(8,128)(2,1)}, u32[]{:S(2)}, u32[]{:S(2)}) collective-permute-start(bf16[64,256]{1,0:T(8,128)(2,1)} %copy.277), channel_id=1, source_target_pairs={{16,0},{18,2},{20,4},{22,6},{24,8},{26,10},{28,12},{30,14},{32,16}... | collective-permute-start | bytes 98312 | tf_op jit(solution)/shard_map/ppermute | solution.py:35
  464.8 51.5 %all-to-all-start.1 = ((f32[2,512,256]{2,1,0:T(8,128)}), f32[2,512,256]{2,1,0:T(8,128)S(1)}, u32[]{:S(2)}, u32[]{:S(2)}) async-start(f32[2,512,256]{2,1,0:T(8,128)} %convolution_bitcast_fusion.2), calls=%async_computation.1 | async-start | bytes 2097152 | tf_op jit(solution)/shard_map/all_to_all | solution.py:52
  478.0 30.2 %collective-permute-start.29 = (bf16[64,256]{1,0:T(8,128)(2,1)}, bf16[64,256]{1,0:T(8,128)(2,1)}, u32[]{:S(2)}, u32[]{:S(2)}) collective-permute-start(bf16[64,256]{1,0:T(8,128)(2,1)} %copy.272), channel_id=1, source_target_pairs={{6,0},{8,2},{10,4},{12,6},{14,8},{16,10},{18,12},{20,14},{22,16},{... | collective-permute-start | bytes 98312 | tf_op jit(solution)/shard_map/ppermute | solution.py:35
  479.3 30.2 %collective-permute-start.28 = (bf16[64,256]{1,0:T(8,128)(2,1)}, bf16[64,256]{1,0:T(8,128)(2,1)}, u32[]{:S(2)}, u32[]{:S(2)}) collective-permute-start(bf16[64,256]{1,0:T(8,128)(2,1)} %copy.271), channel_id=1, source_target_pairs={{4,0},{6,2},{8,4},{10,6},{12,8},{14,10},{16,12},{18,14},{20,16},{2... | collective-permute-start | bytes 98312 | tf_op jit(solution)/shard_map/ppermute | solution.py:35
  480.6 30.2 %collective-permute-start.27 = (bf16[64,256]{1,0:T(8,128)(2,1)}, bf16[64,256]{1,0:T(8,128)(2,1)}, u32[]{:S(2)}, u32[]{:S(2)}) collective-permute-start(bf16[64,256]{1,0:T(8,128)(2,1)} %copy.270), channel_id=1, source_target_pairs={{2,0},{4,2},{6,4},{8,6},{10,8},{12,10},{14,12},{16,14},{18,16},{20... | collective-permute-start | bytes 98312 | tf_op jit(solution)/shard_map/ppermute | solution.py:35
  483.2 28.9 %collective-permute-start.51 = (bf16[64,256]{1,0:T(8,128)(2,1)}, bf16[64,256]{1,0:T(8,128)(2,1)S(1)}, u32[]{:S(2)}, u32[]{:S(2)}) collective-permute-start(bf16[64,256]{1,0:T(8,128)(2,1)} %copy.293), channel_id=1, source_target_pairs={{24,0},{26,2},{28,4},{30,6},{32,8},{34,10},{36,12},{38,14},{40,16}... | collective-permute-start | bytes 98312 | tf_op jit(solution)/shard_map/ppermute | solution.py:35
  484.5 28.9 %collective-permute-start.50 = (bf16[64,256]{1,0:T(8,128)(2,1)}, bf16[64,256]{1,0:T(8,128)(2,1)S(1)}, u32[]{:S(2)}, u32[]{:S(2)}) collective-permute-start(bf16[64,256]{1,0:T(8,128)(2,1)} %copy.292), channel_id=1, source_target_pairs={{22,0},{24,2},{26,4},{28,6},{30,8},{32,10},{34,12},{36,14},{38,16}... | collective-permute-start | bytes 98312 | tf_op jit(solution)/shard_map/ppermute | solution.py:35
  508.2 69.7 %collective-permute-start.49 = (bf16[64,256]{1,0:T(8,128)(2,1)}, bf16[64,256]{1,0:T(8,128)(2,1)S(1)}, u32[]{:S(2)}, u32[]{:S(2)}) collective-permute-start(bf16[64,256]{1,0:T(8,128)(2,1)} %copy.291), channel_id=1, source_target_pairs={{20,0},{22,2},{24,4},{26,6},{28,8},{30,10},{32,12},{34,14},{36,16}... | collective-permute-start | bytes 98312 | tf_op jit(solution)/shard_map/ppermute | solution.py:35
  509.5 69.8 %collective-permute-start.48 = (bf16[64,256]{1,0:T(8,128)(2,1)}, bf16[64,256]{1,0:T(8,128)(2,1)S(1)}, u32[]{:S(2)}, u32[]{:S(2)}) collective-permute-start(bf16[64,256]{1,0:T(8,128)(2,1)} %copy.290), channel_id=1, source_target_pairs={{18,0},{20,2},{22,4},{24,6},{26,8},{28,10},{30,12},{32,14},{34,16}... | collective-permute-start | bytes 98312 | tf_op jit(solution)/shard_map/ppermute | solution.py:35
  510.8 69.8 %collective-permute-start.47 = (bf16[64,256]{1,0:T(8,128)(2,1)}, bf16[64,256]{1,0:T(8,128)(2,1)S(1)}, u32[]{:S(2)}, u32[]{:S(2)}) collective-permute-start(bf16[64,256]{1,0:T(8,128)(2,1)} %copy.289), channel_id=1, source_target_pairs={{16,0},{18,2},{20,4},{22,6},{24,8},{26,10},{28,12},{30,14},{32,16}... | collective-permute-start | bytes 98312 | tf_op jit(solution)/shard_map/ppermute | solution.py:35
  512.1 69.7 %collective-permute-start.46 = (bf16[64,256]{1,0:T(8,128)(2,1)}, bf16[64,256]{1,0:T(8,128)(2,1)S(1)}, u32[]{:S(2)}, u32[]{:S(2)}) collective-permute-start(bf16[64,256]{1,0:T(8,128)(2,1)} %copy.288), channel_id=1, source_target_pairs={{14,0},{16,2},{18,4},{20,6},{22,8},{24,10},{26,12},{28,14},{30,16}... | collective-permute-start | bytes 98312 | tf_op jit(solution)/shard_map/ppermute | solution.py:35
  514.0 69.1 %collective-permute-start.45 = (bf16[64,256]{1,0:T(8,128)(2,1)}, bf16[64,256]{1,0:T(8,128)(2,1)S(1)}, u32[]{:S(2)}, u32[]{:S(2)}) collective-permute-start(bf16[64,256]{1,0:T(8,128)(2,1)} %copy.287), channel_id=1, source_target_pairs={{12,0},{14,2},{16,4},{18,6},{20,8},{22,10},{24,12},{26,14},{28,16}... | collective-permute-start | bytes 98312 | tf_op jit(solution)/shard_map/ppermute | solution.py:35
  516.3 91.4 %all-to-all-start.3 = ((f32[64,4,512]{2,1,0:T(4,128)}), f32[64,4,512]{2,1,0:T(4,128)}, u32[]{:S(2)}, u32[]{:S(2)}) async-start(f32[64,4,512]{2,1,0:T(4,128)} %reduce_sum.134), calls=%async_computation.3 | async-start | bytes 1048576 | tf_op jit(solution)/shard_map/all_to_all | solution.py:59
  577.9 15.4 %collective-permute-start.44 = (bf16[64,256]{1,0:T(8,128)(2,1)}, bf16[64,256]{1,0:T(8,128)(2,1)S(1)}, u32[]{:S(2)}, u32[]{:S(2)}) collective-permute-start(bf16[64,256]{1,0:T(8,128)(2,1)} %copy.286), channel_id=1, source_target_pairs={{10,0},{12,2},{14,4},{16,6},{18,8},{20,10},{22,12},{24,14},{26,16}... | collective-permute-start | bytes 98312 | tf_op jit(solution)/shard_map/ppermute | solution.py:35
  579.2 16.0 %collective-permute-start.43 = (bf16[64,256]{1,0:T(8,128)(2,1)}, bf16[64,256]{1,0:T(8,128)(2,1)S(1)}, u32[]{:S(2)}, u32[]{:S(2)}) collective-permute-start(bf16[64,256]{1,0:T(8,128)(2,1)} %copy.285), channel_id=1, source_target_pairs={{8,0},{10,2},{12,4},{14,6},{16,8},{18,10},{20,12},{22,14},{24,16},... | collective-permute-start | bytes 98312 | tf_op jit(solution)/shard_map/ppermute | solution.py:35
  580.5 16.7 %collective-permute-start.42 = (bf16[64,256]{1,0:T(8,128)(2,1)}, bf16[64,256]{1,0:T(8,128)(2,1)S(1)}, u32[]{:S(2)}, u32[]{:S(2)}) collective-permute-start(bf16[64,256]{1,0:T(8,128)(2,1)} %copy.284), channel_id=1, source_target_pairs={{6,0},{8,2},{10,4},{12,6},{14,8},{16,10},{18,12},{20,14},{22,16},{... | collective-permute-start | bytes 98312 | tf_op jit(solution)/shard_map/ppermute | solution.py:35
  581.9 15.4 %collective-permute-start.41 = (bf16[64,256]{1,0:T(8,128)(2,1)}, bf16[64,256]{1,0:T(8,128)(2,1)S(1)}, u32[]{:S(2)}, u32[]{:S(2)}) collective-permute-start(bf16[64,256]{1,0:T(8,128)(2,1)} %copy.283), channel_id=1, source_target_pairs={{4,0},{6,2},{8,4},{10,6},{12,8},{14,10},{16,12},{18,14},{20,16},{2... | collective-permute-start | bytes 98312 | tf_op jit(solution)/shard_map/ppermute | solution.py:35
  583.2 14.1 %collective-permute-start.40 = (bf16[64,256]{1,0:T(8,128)(2,1)}, bf16[64,256]{1,0:T(8,128)(2,1)S(1)}, u32[]{:S(2)}, u32[]{:S(2)}) collective-permute-start(bf16[64,256]{1,0:T(8,128)(2,1)} %copy.282), channel_id=1, source_target_pairs={{2,0},{4,2},{6,4},{8,6},{10,8},{12,10},{14,12},{16,14},{18,16},{20... | collective-permute-start | bytes 98312 | tf_op jit(solution)/shard_map/ppermute | solution.py:35
  608.6 27.7 %all-to-all-start.6 = ((f32[64,1,1024]{2,1,0:T(1,128)}), f32[64,1,1024]{2,1,0:T(1,128)S(1)}, u32[]{:S(2)}, u32[]{:S(2)}) async-start(f32[64,1,1024]{2,1,0:T(1,128)} %broadcast_in_dim.140), calls=%async_computation.6 | async-start | bytes 524288 | tf_op jit(solution)/shard_map/all_to_all | solution.py:25
  (97 other events, 1884.5 us)
where the time goes:
time: 650 us; the launch traced here: 642 us
  starting transfers between devices  246 us (38%)
  blocking collectives  184 us (28%)
  local copies, waits for them, and re-layouts  79.5 us (12%)
  matrix products  70.4 us (11%)
  other arithmetic  22.8 us (4%)
  waiting for transfers between devices  22.3 us (3%)
  loops' own time  12.8 us (2%)
    all_gather x1, blocking collectives, side_by_side(): out = lax.all_gather(both, axis, axis=dim, tiled=True)  177 us
    ppermute x52, starting transfers between devices, shifted(): return lax.ppermute(block, axis, route)  136 us
    all_to_all x2, starting transfers between devices, sum_by_axis(): return jnp.sum(lax.all_to_all(own, far, 0, 0, tiled=True), axis=0)  83.7 us
    all_to_all x2, starting transfers between devices, sent_to_all(): return lax.all_to_all(copies, axis, split_axis=0, concat_axis=0, tiled=True)  19.3 us
    sub x4, matrix products, attend(): weights = jnp.exp(logit_matrix - row_top)  17.2 us
    convert_element_type x12, local copies, waits for them, and re-layouts, on_device(): portion(window_vg, distance, groups).astype(jnp.bfloat16)  16.7 us
    dot_general x4, matrix products, attend(): jnp.einsum('svu,usc->vsc', rounded_scores, value_tile, preferred_element_...  13.8 us
    ppermute x52, waiting for transfers between devices, shifted(): return lax.ppermute(block, axis, route)  13.5 us
  transfers between devices with their start and end apart: 58, of which 6 were waited for; matrix products, arithmetic and copies ran while one was open for 10% of the time, Pallas kernels for 0%

commit v1 on v0

v1 whole, which is shorter than its diff:
```python
import math
import jax, jax.numpy as jnp
from jax import lax
from jax.experimental import pallas as pl
from jax.experimental.pallas import tpu as pltpu
from jax.sharding import Mesh
from jax.sharding import PartitionSpec as P

F32, BF16 = jnp.float32, jnp.bfloat16
VM = pl.BlockSpec(memory_space=pltpu.VMEM)
SM = pl.BlockSpec(memory_space=pltpu.SMEM)
NEG = -1e30
MIDG = 8
FARG = 128


def dot(a, b):
    return lax.dot_general(a, b, (((1,), (0,)), ((), ())), preferred_element_type=F32)


def dot_nt(a, b):
    return lax.dot_general(a, b, (((1,), (1,)), ((), ())), preferred_element_type=F32)


def fold(x, op):
    return op(x.reshape(x.shape[0] // 8, 8, x.shape[1]), axis=0)


def attention_kernel(q_ref, k_ref, v_ref, g_ref, go_ref, w_ref, rim_ref, win_ref, coarse_ref, keep_ref, frame_ref,
                     att_ref, dq_ref, near_ref, rimg_ref, wing_ref, coarseg_ref, wg_ref,
                     mixed, kaug, vcat, kt, vt, sbuf, dbuf, grads, attT, dqT, qaugT, gT, qm, gm):
    at_ = Place()
    g, s_own, h = at_.plane, at_.shard, at_.h
    p = 4 * g + s_own
    mine = pl.multiple_of(h * 256, 256)
    other = pl.multiple_of((1 - h) * 256, 256)
    mixed[...] = (dot_nt(g_ref[...], w_ref[:, pl.ds(mine, 256)]) + dot_nt(go_ref[...], w_ref[:, pl.ds(other, 256)])).astype(BF16)

    lane = lax.broadcasted_iota(jnp.int32, (16, 128), 1)

    def tile(bias0, bias1):
        return jnp.where(lane == 0, bias0, jnp.where(lane == 1, bias1, 0.0)).astype(BF16)

    def shut(seen):
        return jnp.where(seen, 0.0, NEG).astype(F32)

    first = tile(shut((frame_ref[0] == 1) & (p > 0)), jnp.float32(0.0))
    second = tile(jnp.float32(0.0), shut(frame_ref[1] == 1))
    third = tile(jnp.float32(0.0), jnp.float32(0.0))
    for t in range(16):
        kaug[0, 16 * t:16 * t + 16, 128:256] = first
        kaug[1, 16 * t:16 * t + 16, 128:256] = second
        kaug[2, 16 * t:16 * t + 16, 128:256] = third
    for slot in range(3):
        for k in range(4):
            j = 2 * (k % 2) + k // 2
            at = lax.rem(4 * slot + j - s_own + 12, 12)
            real = p - 12 + at >= 0
            for r in range(4):
                w0 = keep_ref[0, 4 * at + r] == 1
                w1 = keep_ref[1, 4 * at + r] == 1
                if r >= 2:
                    w0 = w0 & (at < 11)
                row = 64 * k + 16 * r
                kaug[3 + slot, row:row + 16, 128:256] = tile(shut(w0 & real), shut(w1 & real))
    rows = lax.broadcasted_iota(jnp.int32, (256, 128), 0)
    lanes = lax.broadcasted_iota(jnp.int32, (256, 128), 1)
    for half in range(2):
        limit = 2 * (2 * p - 1) - 256 * half + 2 * lanes
        kaug[6 + half, :, 128:256] = jnp.where((lanes < 2) & (rows >= limit), NEG, 0.0).astype(BF16)

    @pl.loop(0, 2)
    def _(r):
        lo = pl.multiple_of(r * 128, 128)
        hi = pl.multiple_of(256 + r * 128, 128)
        for ci in range(8):
            if ci == 0:
                kk, vv = rim_ref[:, pl.ds(lo, 128)], rim_ref[:, pl.ds(hi, 128)]
            elif ci < 3:
                kk = k_ref[256 * (ci - 1):256 * ci, pl.ds(lo, 128)]
                vv = v_ref[256 * (ci - 1):256 * ci, pl.ds(lo, 128)]
            elif ci < 6:
                kk = win_ref[256 * (ci - 3):256 * (ci - 2), pl.ds(lo, 128)]
                vv = win_ref[256 * (ci - 3):256 * (ci - 2), pl.ds(hi, 128)]
            else:
                kk = coarse_ref[256 * (ci - 6):256 * (ci - 5), pl.ds(lo, 128)]
                vv = coarse_ref[256 * (ci - 6):256 * (ci - 5), pl.ds(hi, 128)]
            kaug[ci, :, 0:128] = kk
            vcat[ci] = vv
            kt[ci] = kk.T
            vt[ci] = vv.T
        sub = lax.broadcasted_iota(jnp.int32, (128, 256), 0)
        lan = lax.broadcasted_iota(jnp.int32, (256, 128), 1)
        subq = lax.broadcasted_iota(jnp.int32, (128, 512), 0)
        causal_row = lax.broadcasted_iota(jnp.int32, (256, 512), 0)
        causal_q = lax.broadcasted_iota(jnp.int32, (256, 512), 1) % 256
        zero = jnp.zeros((), BF16)
        for b in range(2):
            qp = q_ref[256 * b:256 * b + 256, pl.ds(lo, 128)] * jnp.asarray(0.125, BF16)
            gp = mixed[256 * b:256 * b + 256, pl.ds(lo, 128)]
            qt, gt = qp.T, gp.T
            for head in range(2):
                keep_t = (sub // 64) == head
                keep_l = (lan // 64) == head
                qaugT[0:128, 256 * head:256 * head + 256] = jnp.where(keep_t, qt, zero)
                gT[:, 256 * head:256 * head + 256] = jnp.where(keep_t, gt, zero)
                qm[256 * head:256 * head + 256, :] = jnp.where(keep_l, qp, zero)
                gm[256 * head:256 * head + 256, :] = jnp.where(keep_l, gp, zero)
            qaugT[128:256, :] = jnp.where(subq == b, 1.0, 0.0).astype(BF16)
            chunks = [b, b + 1, 3, 4, 5, 6, 7]
            top = jnp.full((8, 512), NEG, F32)
            for n, ci in enumerate(chunks):
                sc = dot(kaug[ci], qaugT[...])
                if n == 1:
                    sc = jnp.where(causal_row <= causal_q, sc, NEG)
                sbuf[n] = sc
                top = jnp.maximum(top, fold(sc, jnp.max))
            top = jnp.max(top, axis=0, keepdims=True)
            total = jnp.zeros((8, 512), F32)
            centre = jnp.zeros((8, 512), F32)
            for n, ci in enumerate(chunks):
                e = jnp.exp(sbuf[n] - top)
                dp = dot(vcat[ci], gT[...])
                sbuf[n] = e
                dbuf[n] = dp
                total = total + fold(e, jnp.sum)
                centre = centre + fold(e * dp, jnp.sum)
            inv = 1.0 / jnp.sum(total, axis=0, keepdims=True)
            centre = jnp.sum(centre, axis=0, keepdims=True) * inv
            oT = [jnp.zeros((64, 256), F32)] * 2
            qT = [jnp.zeros((64, 256), F32)] * 2
            for n, ci in enumerate(chunks):
                share = sbuf[n] * inv
                pr = share.astype(BF16)
                ds = (share * (dbuf[n] - centre)).astype(BF16)
                dk = dot(ds, qm[...])
                dv = dot(pr, gm[...])
                if b == 1 and ci != 2:
                    grads[ci, :, 0:128] += dk
                    grads[ci, :, 128:256] += dv
                else:
                    grads[ci, :, 0:128] = dk
                    grads[ci, :, 128:256] = dv
                for head in range(2):
                    oT[head] = oT[head] + dot(vt[ci, 64 * head:64 * head + 64, :], pr[:, 256 * head:256 * head + 256])
                    qT[head] = qT[head] + dot(kt[ci, 64 * head:64 * head + 64, :], ds[:, 256 * head:256 * head + 256])
            for head in range(2):
                attT[r, 64 * head:64 * head + 64, 256 * b:256 * b + 256] = oT[head].astype(BF16)
                dqT[r, 64 * head:64 * head + 64, 256 * b:256 * b + 256] = (qT[head] * 0.125).astype(BF16)
        for part, where in ((0, lo), (1, hi)):
            cols = slice(128 * part, 128 * part + 128)
            rimg_ref[:, pl.ds(where, 128)] = grads[0, :, cols].astype(BF16)
            for ci in (1, 2):
                near_ref[256 * (ci - 1):256 * ci, pl.ds(where, 128)] = grads[ci, :, cols]
            for ci in (3, 4, 5):
                wing_ref[256 * (ci - 3):256 * (ci - 2), pl.ds(where, 128)] = grads[ci, :, cols].astype(BF16)
            for ci in (6, 7):
                coarseg_ref[256 * (ci - 6):256 * (ci - 5), pl.ds(where, 128)] = grads[ci, :, cols].astype(BF16)
        att_ref[:, pl.ds(lo, 128)] = attT[r].T
        dq_ref[:, pl.ds(lo, 128)] = dqT[r].T

    scale = 1.0 / 256.0
    at = attT[...].reshape(256, 512)
    wg_ref[:, pl.ds(mine, 256)] = (dot(at, g_ref[...]) * scale).astype(BF16)
    wg_ref[:, pl.ds(other, 256)] = (dot(at, go_ref[...]) * scale).astype(BF16)


def attention(*args):
    return pl.pallas_call(
        attention_kernel,
        out_shape=[
            jax.ShapeDtypeStruct((512, 256), BF16), jax.ShapeDtypeStruct((512, 256), BF16),
            jax.ShapeDtypeStruct((512, 512), F32), jax.ShapeDtypeStruct((256, 512), BF16),
            jax.ShapeDtypeStruct((768, 512), BF16), jax.ShapeDtypeStruct((512, 512), BF16),
            jax.ShapeDtypeStruct((256, 512), BF16)],
        in_specs=[VM] * 9 + [SM] * 2,
        out_specs=[VM] * 7,
        scratch_shapes=[
            pltpu.VMEM((512, 256), BF16), pltpu.VMEM((8, 256, 256), BF16), pltpu.VMEM((8, 256, 128), BF16),
            pltpu.VMEM((8, 128, 256), BF16), pltpu.VMEM((8, 128, 256), BF16),
            pltpu.VMEM((7, 256, 512), F32), pltpu.VMEM((7, 256, 512), F32), pltpu.VMEM((8, 256, 256), F32),
            pltpu.VMEM((2, 128, 512), BF16), pltpu.VMEM((2, 128, 512), BF16),
            pltpu.VMEM((256, 512), BF16), pltpu.VMEM((128, 512), BF16),
            pltpu.VMEM((512, 128), BF16), pltpu.VMEM((512, 128), BF16)],
        compiler_params=pltpu.CompilerParams(vmem_limit_bytes=48 * 2**20),
        name="attention",
    )(*args)


MESH = pl.DeviceIdType.MESH


class Place:
    def __init__(self):
        self.x, self.z = lax.axis_index("x"), lax.axis_index("z")
        self.yh, self.c, self.h = lax.axis_index("yh"), lax.axis_index("c"), lax.axis_index("h")
        self.plane = 8 * self.x + self.z
        self.shard = 2 * self.yh + self.c
        self.core = {"c": 1 - self.c}
        self.far = {"yh": 1 - self.yh}
        self.diagonal = {"yh": 1 - self.yh, "c": 1 - self.c}
        self.head = {"h": 1 - self.h}

    def along_z(self, i):
        return lax.rem(self.z + i, 8)

    def along_x(self, i):
        return lax.rem(self.x + i, 4)

    def next_plane(self, step):
        to = lax.rem(self.plane + step + 32, 32)
        return {"x": to // 8, "z": lax.rem(to, 8)}

    def next_shard(self, step):
        to = lax.rem(4 * self.plane + self.shard + step + 128, 128)
        return {"x": to // 32, "z": lax.rem(to // 4, 8), "yh": lax.rem(to // 2, 2), "c": lax.rem(to, 2)}

    def greet(self, diagonal):
        peers = [self.core, self.far, self.head, self.next_plane(1), self.next_plane(-1), self.next_shard(1), self.next_shard(-1)]
        peers += [{"z": self.along_z(i)} for i in range(1, 8)]
        peers += [{"x": self.along_x(i)} for i in range(1, 4)]
        if diagonal:
            peers.append(self.diagonal)
        barrier = pltpu.get_barrier_semaphore()
        for peer in peers:
            pl.semaphore_signal(barrier, inc=1, device_id=peer, device_id_type=MESH)
        return barrier, len(peers)


class Mail:
    def __init__(self, send_sems, recv_sems):
        self.sems, self.used, self.all = (send_sems, recv_sems), 0, []

    def send(self, source, target, device):
        at = self.used
        self.used += 1
        copy = pltpu.make_async_remote_copy(
            src_ref=source, dst_ref=target, send_sem=self.sems[0].at[at], recv_sem=self.sems[1].at[at],
            device_id=device, device_id_type=MESH)
        copy.start()
        self.all.append(copy)
        return copy

    def finish(self):
        for copy in self.all:
            copy.wait_send()


def gather_kernel(k_ref, v_ref, g_ref, w_ref, rim_ref, win_ref, coarse_ref, go_ref, wo_ref, pooled, last, send_sems, recv_sems):
    at = Place()
    barrier, count = at.greet(False)
    row = lax.broadcasted_iota(jnp.int32, (80, 512), 0)
    token = lax.broadcasted_iota(jnp.int32, (80, 512), 1)
    group = jnp.where(row < 64, token // MIDG, 128 + token // FARG)
    owner = jnp.where(row < 64, row, 128 + (row - 64) - 4 * at.shard)
    ones = jnp.where(owner == group, 1.0, 0.0).astype(BF16)
    kind = lax.broadcasted_iota(jnp.int32, (80, 256), 0)
    me = 2 * at.c + at.yh
    pooled[me, :, 0:256] = (dot(ones, k_ref[...]) / jnp.where(kind < 64, math.sqrt(MIDG), math.sqrt(FARG))).astype(BF16)
    pooled[me, :, 256:512] = (dot(ones, v_ref[...]) / jnp.where(kind < 64, float(MIDG), float(FARG))).astype(BF16)
    pl.semaphore_wait(barrier, count)

    mail = Mail(send_sems, recv_sems)
    pair = pl.ds(2 * at.c, 2)
    far = mail.send(pooled.at[me], pooled.at[me], at.far)
    rim = [mail.send(k_ref.at[256:512, :], rim_ref.at[:, 0:256], at.next_shard(1)),
           mail.send(v_ref.at[256:512, :], rim_ref.at[:, 256:512], at.next_shard(1))]
    heads = [mail.send(g_ref, go_ref, at.head),
             mail.send(w_ref.at[:, pl.ds(pl.multiple_of(256 * (1 - at.h), 256), 256)], wo_ref, at.head)]
    far.wait_recv()
    beside = mail.send(pooled.at[pair], pooled.at[pair], at.core)
    ahead = at.next_plane(1)
    hop1 = mail.send(pooled.at[pair, 0:64, :], win_ref.at[2, pair], ahead)
    beside.wait_recv()
    half = pl.ds(pl.multiple_of(256 * at.c, 256), 256)
    total = pooled[0, 64:80, half].astype(F32)
    for n in range(1, 4):
        total = total + pooled[n, 64:80, half].astype(F32)
    coarse_ref[at.plane, :, half] = total.astype(BF16)
    mine = coarse_ref.at[at.plane, :, half]
    over_z = [mail.send(mine, mine, {"z": at.along_z(i)}) for i in range(1, 8)]
    hop1.wait_recv()
    hop2 = mail.send(win_ref.at[2, pair], win_ref.at[1, pair], ahead)
    share1 = mail.send(win_ref.at[2, pair], win_ref.at[2, pair], at.core)
    for copy in over_z:
        copy.wait_recv()
    line = coarse_ref.at[pl.ds(8 * at.x, 8), :, half]
    over_x = [mail.send(line, line, {"x": at.along_x(i)}) for i in range(1, 4)]
    hop2.wait_recv()
    hop3 = mail.send(win_ref.at[1, pair], last.at[pair], ahead)
    share2 = mail.send(win_ref.at[1, pair], win_ref.at[1, pair], at.core)
    for copy in over_x:
        copy.wait_recv()
    whole = coarse_ref.at[:, :, half]
    share_coarse = mail.send(whole, whole, at.core)
    hop3.wait_recv()
    share3 = mail.send(last.at[pair], last.at[pair], at.core)
    share3.wait_recv()
    for n in range(4):
        old = 2 * (n % 2) + n // 2 >= at.shard
        win_ref[0, n] = jnp.where(old, last[n], pooled[n, 0:64, :])
    for copy in [share1, share2, share_coarse] + rim + heads:
        copy.wait_recv()
    mail.finish()


def gather(k, v, g, w):
    return pl.pallas_call(
        gather_kernel,
        out_shape=[
            jax.ShapeDtypeStruct((256, 512), BF16), jax.ShapeDtypeStruct((3, 4, 64, 512), BF16),
            jax.ShapeDtypeStruct((32, 16, 512), BF16), jax.ShapeDtypeStruct((512, 256), BF16),
            jax.ShapeDtypeStruct((256, 256), BF16)],
        in_specs=[VM] * 4,
        out_specs=[VM] * 5,
        scratch_shapes=[
            pltpu.VMEM((4, 80, 512), BF16), pltpu.VMEM((4, 64, 512), BF16),
            pltpu.SemaphoreType.DMA((23,)), pltpu.SemaphoreType.DMA((23,))],
        compiler_params=pltpu.CompilerParams(collective_id=0, has_side_effects=True, vmem_limit_bytes=32 * 2**20),
        name="gather",
    )(k, v, g, w)


def reduce_kernel(att_ref, near_ref, rimg_ref, wing_ref, cg_ref, wg_ref, w_ref, wo_ref,
                  out_ref, kg_ref, vg_ref, weight_ref,
                  atto, rimr, winr, coarser, wgr, wx, wxr, wz, wzr, wfar, wmine, wall, cx, cxr, cz, czr, cp, cpr, cfull,
                  acc, hops, hopr, midb, midr, send_sems, recv_sems):
    at = Place()
    barrier, count = at.greet(True)
    pl.semaphore_wait(barrier, count)
    mail = Mail(send_sems, recv_sems)
    c, x, z, yh = at.c, at.x, at.z, at.yh

    def lanes(n):
        return pl.ds(pl.multiple_of(256 * n, 256), 256)

    def up(value):
        return value.astype(F32)

    to_w = mail.send(wg_ref.at[pl.ds(pl.multiple_of(128 * (1 - c), 128), 128), :], wgr, at.core)
    to_win = mail.send(wing_ref.at[:, pl.ds(2 * (1 - c), 2)], winr, at.core)
    to_c = mail.send(cg_ref.at[:, :, lanes(1 - c)], coarser, at.core)
    to_att = mail.send(att_ref, atto, at.head)
    to_rim = mail.send(rimg_ref, rimr, at.next_shard(-1))

    to_w.wait_recv()
    wx[...] = (up(wg_ref[pl.ds(pl.multiple_of(128 * c, 128), 128), :]) + up(wgr[...])).astype(BF16).reshape(4, 32, 512)
    to_wx = [mail.send(wx.at[at.along_x(i)], wxr.at[i - 1], {"x": at.along_x(i)}) for i in range(1, 4)]

    to_win.wait_recv()
    shard, beside = at.shard, 2 * yh + 1 - c
    for n in range(2):
        j = 2 * n + c
        own, got = up(wing_ref[0, 2 * c + n]), up(winr[0, n])
        hops[0, n] = (jnp.where(j >= shard, own, 0.0) + jnp.where(j >= beside, got, 0.0)).astype(BF16)
        acc[2, n] = jnp.where(j >= shard, 0.0, own) + jnp.where(j >= beside, 0.0, got)
    back = at.next_plane(-1)
    hop = [mail.send(hops.at[0], hopr.at[0], back)]
    for m in range(2):
        acc[m] = up(wing_ref[1 + m, pl.ds(2 * c, 2)]) + up(winr[1 + m])

    to_c.wait_recv()
    cx[...] = (up(cg_ref[:, :, lanes(c)]) + up(coarser[...])).astype(BF16)
    to_cx = [mail.send(cx.at[pl.ds(8 * at.along_x(i), 8)], cxr.at[i - 1], {"x": at.along_x(i)}) for i in range(1, 4)]

    for copy in to_wx:
        copy.wait_recv()
    total = up(wx[x])
    for i in range(3):
        total = total + up(wxr[i])
    for n in range(8):
        wz[n] = total[16 * (n // 4):16 * (n // 4) + 16, 128 * (n % 4):128 * (n % 4) + 128].astype(BF16)
    to_wz = [mail.send(wz.at[at.along_z(i)], wzr.at[i - 1], {"z": at.along_z(i)}) for i in range(1, 8)]

    for copy in to_cx:
        copy.wait_recv()
    total = up(cx[pl.ds(8 * x, 8)])
    for i in range(3):
        total = total + up(cxr[i])
    cz[...] = total.astype(BF16)
    to_cz = [mail.send(cz.at[at.along_z(i)], czr.at[i - 1], {"z": at.along_z(i)}) for i in range(1, 8)]

    hop[0].wait_recv()
    hops[1] = (up(hopr[0]) + acc[0]).astype(BF16)
    hop.append(mail.send(hops.at[1], hopr.at[1], back))

    for copy in to_wz:
        copy.wait_recv()
    total = up(wz[z])
    for i in range(7):
        total = total + up(wzr[i])
    wmine[...] = total
    to_far = mail.send(wmine, wfar, at.far)

    for copy in to_cz:
        copy.wait_recv()
    total = up(cz[z])
    for i in range(7):
        total = total + up(czr[i])
    cp[...] = total.astype(BF16)
    to_cp = [mail.send(cp, cpr.at[n], peer) for n, peer in enumerate((at.far, at.core, at.diagonal))]

    hop[1].wait_recv()
    hops[2] = (up(hopr[1]) + acc[1]).astype(BF16)
    hop.append(mail.send(hops.at[2], hopr.at[2], back))

    to_far.wait_recv()
    wall[z] = wmine[...] + wfar[...]
    to_wall = [mail.send(wall.at[z], wall.at[z], {"z": at.along_z(i)}) for i in range(1, 8)]

    to_att.wait_recv()
    out_ref[...] = (dot(att_ref[...], w_ref[:, lanes(at.h)]) + dot(atto[...], wo_ref[...])).astype(BF16)

    for copy in to_wall:
        copy.wait_recv()
    for n in range(8):
        weight_ref[c, x, 16 * (n // 4):16 * (n // 4) + 16, 128 * (n % 4):128 * (n % 4) + 128] = wall[n]
    line = weight_ref.at[c, x]
    to_line = [mail.send(line, line, {"x": at.along_x(i)}) for i in range(1, 4)]

    hop[2].wait_recv()
    acc[0] = up(hopr[2]) + acc[2]
    midb[...] = acc[0, 1 - yh].astype(BF16)
    to_mid = mail.send(midb, midr, at.far)

    for copy in to_cp:
        copy.wait_recv()
    cfull[:, lanes(c)] = up(cp[...]) + up(cpr[0])
    cfull[:, lanes(1 - c)] = up(cpr[1]) + up(cpr[2])
    to_rim.wait_recv()

    for copy in to_line:
        copy.wait_recv()
    to_half = mail.send(weight_ref.at[c], weight_ref.at[c], at.core)

    to_mid.wait_recv()
    mid = acc[0, yh] + up(midr[...])
    token = lax.broadcasted_iota(jnp.int32, (512, 80), 0)
    row = lax.broadcasted_iota(jnp.int32, (512, 80), 1)
    spread = jnp.where(jnp.where(row < 64, token // MIDG, 64 + 4 * at.shard + token // FARG) == row, 1.0, 0.0).astype(BF16)
    for n, target, mid_div, far_div in ((0, kg_ref, math.sqrt(MIDG), math.sqrt(FARG)), (1, vg_ref, float(MIDG), float(FARG))):
        cols = slice(256 * n, 256 * n + 256)
        pools = jnp.concatenate([mid[:, cols] / mid_div, cfull[:, cols] / far_div], axis=0)
        high = pools.astype(BF16)
        low = (pools - up(high)).astype(BF16)
        added = dot(spread, high) + dot(spread, low) + near_ref[:, cols]
        target[0:256, :] = added[0:256].astype(BF16)
        target[256:512, :] = (added[256:512] + up(rimr[:, cols])).astype(BF16)
    to_half.wait_recv()
    mail.finish()


def reduce(att, near, rimg, wing, cg, wg, w, wo):
    B, S = (lambda *s: pltpu.VMEM(s, BF16)), (lambda *s: pltpu.VMEM(s, F32))
    return pl.pallas_call(
        reduce_kernel,
        out_shape=[
            jax.ShapeDtypeStruct((512, 256), BF16), jax.ShapeDtypeStruct((512, 256), BF16),
            jax.ShapeDtypeStruct((512, 256), BF16), jax.ShapeDtypeStruct((2, 4, 32, 512), F32)],
        in_specs=[VM] * 8,
        out_specs=[VM] * 4,
        scratch_shapes=[
            B(512, 256), B(256, 512), B(3, 2, 64, 512), B(32, 16, 256), B(128, 512),
            B(4, 32, 512), B(3, 32, 512), B(8, 16, 128), B(7, 16, 128), S(16, 128), S(16, 128), S(8, 16, 128),
            B(32, 16, 256), B(3, 8, 16, 256), B(8, 16, 256), B(7, 16, 256), B(16, 256), B(3, 16, 256), S(16, 512),
            S(3, 2, 64, 512), B(3, 2, 64, 512), B(3, 2, 64, 512), B(64, 512), B(64, 512),
            pltpu.SemaphoreType.DMA((44,)), pltpu.SemaphoreType.DMA((44,))],
        compiler_params=pltpu.CompilerParams(collective_id=1, has_side_effects=True, vmem_limit_bytes=40 * 2**20),
        name="reduce",
    )(att, near, rimg, wing, cg, wg, w, wo)


def on_device(queries, key_vectors, value_vectors, out_grad, out_weight, mid_keep, frame_keep):
    rim, win, coarse, other_grad, other_weight = gather(key_vectors, value_vectors, out_grad, out_weight)
    att, dq, near, rimg, wing, cg, wg = attention(
        queries, key_vectors, value_vectors, out_grad, other_grad, out_weight,
        rim, win.reshape(768, 512), coarse.reshape(512, 512), mid_keep, frame_keep)
    output, kg, vg, weight = reduce(
        att, near, rimg, wing.reshape(3, 4, 64, 512), cg.reshape(32, 16, 512), wg, out_weight, other_weight)
    return output, dq, kg, vg, weight.reshape(256, 512)


def solution(mesh):
    split = Mesh(mesh.devices.reshape(4, 8, 2, 2, 2), ("x", "z", "yh", "c", "h"))
    seq = ("x", "z", "yh", "c")
    return jax.shard_map(
        on_device,
        mesh=split,
        in_specs=(P(seq, "h"), P(seq, "h"), P(seq, "h"), P(seq, "h"), P("h", None), P(seq, None), P(seq)),
        out_specs=(P(seq, "h"), P(seq, "h"), P(seq, "h"), P(seq, "h"), P("h", None)),
        check_vma=False,
    )
```

time: 650 us -> 98.6 us (0.15); the launches traced: 642 us -> 98.3 us
  starting transfers between devices: 246 us -> 0 us
  blocking collectives: 184 us -> 0 us
  Pallas kernels: 0 us -> 88.1 us
  matrix products: 70.4 us -> 0 us
  local copies, waits for them, and re-layouts: 79.5 us -> 9.51 us
  other arithmetic: 22.8 us -> 0 us
  waiting for transfers between devices: 22.3 us -> 0 us
  loops' own time: 12.8 us -> 0 us
    all_gather x1 -> x0, blocking collectives: 177 us -> none  [side_by_side(): out = lax.all_gather(both, axis, axis=dim, tiled=True)]
    ppermute x52 -> x0, starting transfers between devices: 136 us -> none  [shifted(): return lax.ppermute(block, axis, route)]
    all_to_all x6 -> x0, starting transfers between devices: 111 us -> none  [the longest x2 83.7 us: sum_by_axis(): return jnp.sum(lax.all_to_all(own, far, 0, 0, tiled=True), axis=0)]
    pallas_call x0 -> x3, Pallas kernels: none -> 88.1 us  [the longest x1 35.6 us: reduce(): pl.pallas_call(reduce_kernel, out_shape=[jax.ShapeDtypeStruct((512, 256),...]
    dot_general x23 -> x0, matrix products: 53.2 us -> none  [the longest x4 13.8 us: attend(): jnp.einsum('svu,usc->vsc', rounded_scores, value_tile, preferred_element_...]
    convert_element_type x24 -> x0, local copies, waits for them, and re-layouts: 25 us -> none  [the longest x12 16.7 us: on_device(): portion(window_vg, distance, groups).astype(jnp.bfloat16)]
    sub x4 -> x0, matrix products: 17.2 us -> none  [attend(): weights = jnp.exp(logit_matrix - row_top)]
    ppermute x52 -> x0, waiting for transfers between devices: 13.5 us -> none  [shifted(): return lax.ppermute(block, axis, route)]
  transfers between devices with their start and end apart: 58 -> 0, of which waited for: 6 -> 0; matrix products, arithmetic and copies ran while one was open for 10% -> 0% of each run, Pallas kernels for 0% -> 0%
where the time goes in v1:
time: 98.6 us; the launch traced here: 98.3 us
  Pallas kernels  88.1 us (89%)
  local copies, waits for them, and re-layouts  9.51 us (10%)
    pallas_call x1, Pallas kernels, reduce(): pl.pallas_call(reduce_kernel, out_shape=[jax.ShapeDtypeStruct((512, 256),...  35.6 us
    pallas_call x1, Pallas kernels, gather(): pl.pallas_call(gather_kernel, out_shape=[jax.ShapeDtypeStruct((256, 512),...  35.5 us
    pallas_call x1, Pallas kernels, attention(): pl.pallas_call(attention_kernel, out_shape=[jax.ShapeDtypeStruct((512, 25...  17 us
    unnamed x28, local copies, waits for them, and re-layouts  9.51 us

profile of v1, /device:TPU:1, one launch (start us, length us, event | category | flops | bytes accessed | tf_op | source)
XLA Modules:
  0.0 98.3 jit_solution(8454438230950116351)
XLA Ops:
  0.6 0.0 copy-start
  0.6 0.9 copy-done
  1.6 0.0 copy-start.3
  1.6 0.9 copy-done.3
  2.5 0.0 copy-start.5
  2.5 0.9 copy-done.5
  3.5 0.0 copy-start.7
  3.5 0.9 copy-done.7
  4.4 0.0 copy-start.1
  4.4 0.0 copy-start.4
  4.4 0.0 copy-start.6
  4.4 0.0 copy-start.8
  4.4 35.5 %gather.1 = (bf16[256,512]{1,0:T(8,128)(2,1)S(1)}, bf16[3,4,64,512]{3,2,1,0:T(8,128)(2,1)S(1)}, bf16[32,16,512]{2,1,0:T(8,128)(2,1)S(1)}, bf16[512,256]{1,0:T(8,128)(2,1)S(1)}, bf16[256,256]{1,0:T(8,128)(2,1)S(1)}) custom-call(bf16[512,256]{1,0:T(8,128)(2,1)S(1)} %copy-done.3, bf16[512,256]{1,0:T(8,128)(2,1)S(1)} %copy-done.5, ...), custom_call_target="tpu_custom_call" | custom-call | tf_op jit(solution)/shard_map/gather/pallas_call | solution.py:308
  39.9 0.0 copy-start.10
  40.0 0.0 copy-start.11
  40.0 0.0 copy-done.1
  40.0 0.0 copy-done.4
  40.0 0.0 copy-done.6
  40.0 0.0 copy-done.8
  40.0 0.6 copy-done.10
  40.6 0.0 copy-done.11
  40.6 0.0 copy-start.9
  40.6 0.9 copy-done.9
  41.6 17.0 %attention.1 = (bf16[512,256]{1,0:T(8,128)(2,1)S(1)}, bf16[512,256]{1,0:T(8,128)(2,1)}, f32[512,512]{1,0:T(8,128)}, bf16[256,512]{1,0:T(8,128)(2,1)S(1)}, bf16[7...) custom-call(bf16[512,256]{1,0:T(8,128)(2,1)S(1)} %copy-done.9, ...), custom_call_target="tpu_custom_call" | custom-call | tf_op jit(solution)/shard_map/attention/pallas_call | solution.py:169
  58.6 0.0 copy-start.2
  58.6 1.2 %copy-done.2 = f32[512,512]{1,0:T(8,128)S(1)} copy-done((f32[512,512]{1,0:T(8,128)S(1)}, f32[512,512]{1,0:T(8,128)}, u32[]{:S(2)}) %copy-start.2) | copy-done | bytes 1048600
  59.8 35.6 %reduce.1 = (bf16[512,256]{1,0:T(8,128)(2,1)S(1)}, bf16[512,256]{1,0:T(8,128)(2,1)S(1)}, bf16[512,256]{1,0:T(8,128)(2,1)S(1)}, f32[2,4,32,512]{3,2,1,0:T(8,128)S(1)}) custom-call(bf16[512,256]{1,0:T(8,128)(2,1)S(1)} %get-tuple-element.25.att_ref, f32[512,512]{1,0:T(8,128)S(1)} %copy-done.2, bf16[256,512]{1,0:T(8,128)(2,1)S(1)} %get-tuple-element.27.rimg_ref, ...), custom_call_target="tpu_custom_call" | custom-call | tf_op jit(solution)/shard_map/reduce/pallas_call | solution.py:455
  95.4 0.7 copy.16
  96.1 0.7 copy.17
  96.8 0.7 copy.18
  97.5 0.8 copy.19
Async XLA Ops:
  0.6 1.0 copy-start
  1.6 0.9 copy-start.3
  2.5 0.9 copy-start.5
  3.5 0.9 copy-start.7
  4.4 35.5 %copy-start.1 = (bf16[256,512]{1,0:T(8,128)(2,1)S(1)}, bf16[256,512]{1,0:T(8,128)(2,1)}, u32[]{:S(2)}) copy-start(bf16[256,512]{1,0:T(8,128)(2,1)} %w_ref.5) | copy-start | bytes 786436
  4.4 35.5 %copy-start.4 = (bf16[512,256]{1,0:T(8,128)(2,1)S(1)}, bf16[512,256]{1,0:T(8,128)(2,1)}, u32[]{:S(2)}) copy-start(bf16[512,256]{1,0:T(8,128)(2,1)} %k_ref.3) | copy-start | bytes 786436
  4.4 35.6 %copy-start.6 = (bf16[512,256]{1,0:T(8,128)(2,1)S(1)}, bf16[512,256]{1,0:T(8,128)(2,1)}, u32[]{:S(2)}) copy-start(bf16[512,256]{1,0:T(8,128)(2,1)} %v_ref.3) | copy-start | bytes 786436
  4.4 35.6 %copy-start.8 = (bf16[512,256]{1,0:T(8,128)(2,1)S(1)}, bf16[512,256]{1,0:T(8,128)(2,1)}, u32[]{:S(2)}) copy-start(bf16[512,256]{1,0:T(8,128)(2,1)} %g_ref.3) | copy-start | bytes 786436
  39.9 0.7 copy-start.10
  40.0 0.7 copy-start.11
  40.6 1.0 copy-start.9
  58.6 1.2 %copy-start.2 = (f32[512,512]{1,0:T(8,128)S(1)}, f32[512,512]{1,0:T(8,128)}, u32[]{:S(2)}) copy-start(f32[512,512]{1,0:T(8,128)} %get-tuple-element.26.near_ref) | copy-start | bytes 3145732

commit v2 on v1

v2 whole, which is shorter than its diff:
```python
import math

import jax
import jax.numpy as jnp
from jax import lax
from jax.experimental import pallas as pl
from jax.experimental.pallas import tpu as pltpu
from jax.sharding import Mesh
from jax.sharding import PartitionSpec as P

F32, BF16 = jnp.float32, jnp.bfloat16
VM = pl.BlockSpec(memory_space=pltpu.VMEM)
SM = pl.BlockSpec(memory_space=pltpu.SMEM)
ANY = pl.BlockSpec(memory_space=pl.ANY)
NEG = -1e30
MIDG = 8
FARG = 128


def dot(a, b):
    return lax.dot_general(a, b, (((1,), (0,)), ((), ())), preferred_element_type=F32)


def dot_nt(a, b):
    return lax.dot_general(a, b, (((1,), (1,)), ((), ())), preferred_element_type=F32)


def fold(x, op):
    return op(x.reshape(x.shape[0] // 8, 8, x.shape[1]), axis=0)


def up(value):
    return value.astype(F32)


MESH = pl.DeviceIdType.MESH


class Place:
    def __init__(self):
        self.x, self.z = lax.axis_index("x"), lax.axis_index("z")
        self.yh, self.c, self.h = lax.axis_index("yh"), lax.axis_index("c"), lax.axis_index("h")
        self.plane = 8 * self.x + self.z
        self.shard = 2 * self.yh + self.c
        self.core = {"c": 1 - self.c}
        self.far = {"yh": 1 - self.yh}
        self.diagonal = {"yh": 1 - self.yh, "c": 1 - self.c}
        self.head = {"h": 1 - self.h}

    def along_z(self, i):
        return lax.rem(self.z + i, 8)

    def along_x(self, i):
        return lax.rem(self.x + i, 4)

    def next_plane(self, step):
        to = lax.rem(self.plane + step + 32, 32)
        return {"x": to // 8, "z": lax.rem(to, 8)}

    def next_shard(self, step):
        to = lax.rem(4 * self.plane + self.shard + step + 128, 128)
        return {"x": to // 32, "z": lax.rem(to // 4, 8), "yh": lax.rem(to // 2, 2), "c": lax.rem(to, 2)}

    def greet(self, diagonal):
        peers = [self.core, self.far, self.head, self.next_plane(1), self.next_plane(-1), self.next_shard(1), self.next_shard(-1)]
        peers += [{"z": self.along_z(i)} for i in range(1, 8)]
        peers += [{"x": self.along_x(i)} for i in range(1, 4)]
        if diagonal:
            peers.append(self.diagonal)
        barrier = pltpu.get_barrier_semaphore()
        for peer in peers:
            pl.semaphore_signal(barrier, inc=1, device_id=peer, device_id_type=MESH)
        return barrier, len(peers)


class Mail:
    def __init__(self, send_sems, recv_sems):
        self.sems, self.used, self.all = (send_sems, recv_sems), 0, []

    def send(self, source, target, device):
        at = self.used
        self.used += 1
        copy = pltpu.make_async_remote_copy(
            src_ref=source, dst_ref=target, send_sem=self.sems[0].at[at], recv_sem=self.sems[1].at[at],
            device_id=device, device_id_type=MESH)
        copy.start()
        self.all.append(copy)
        return copy

    def finish(self):
        for copy in self.all:
            copy.wait_send()


def layer_kernel(q_hbm, k_hbm, v_hbm, g_hbm, w_hbm, keep_ref, frame_ref,
                 out_ref, dq_ref, kg_ref, vg_ref, weight_ref,
                 q, k, v, g, w, rim, go, wo, pooled, win, last, coarse, mixed,
                 kaug, vcat, kt, vt, qaugT, gT, qm, gm, sbuf, dbuf, pbuf, tops, stats,
                 attT, att, atto, dqT, wg, wgb, wgr, wx, wxr, wz, wzr, wall,
                 near, rimg, rimr, wing, winr, acc, hops, hopr, mid, midb, midr,
                 cg, cr, cx, cxr, cz, czr, cp, cpr, cfull,
                 load_sems, send_sems, recv_sems):
    at = Place()
    c, x, z, yh, h, shard = at.c, at.x, at.z, at.yh, at.h, at.shard
    p = 4 * at.plane + shard
    loads = [pltpu.make_async_copy(a, b, load_sems.at[n])
             for n, (a, b) in enumerate(((k_hbm, k), (v_hbm, v), (g_hbm, g), (w_hbm, w), (q_hbm, q)))]
    for load in loads:
        load.start()
    barrier, count = at.greet(True)

    def lanes(n, size=256):
        return pl.ds(pl.multiple_of(size * n, size), size)

    row = lax.broadcasted_iota(jnp.int32, (80, 512), 0)
    token = lax.broadcasted_iota(jnp.int32, (80, 512), 1)
    owner = jnp.where(row < 64, row, 128 + (row - 64) - 4 * shard)
    group = jnp.where(row < 64, token // MIDG, 128 + token // FARG)
    ones = jnp.where(owner == group, 1.0, 0.0).astype(BF16)
    kind = lax.broadcasted_iota(jnp.int32, (80, 256), 0)
    me, peer = 2 * c + yh, 2 * c + 1 - yh
    loads[0].wait()
    pooled[me, :, 0:256] = (dot(ones, k[...]) / jnp.where(kind < 64, math.sqrt(MIDG), math.sqrt(FARG))).astype(BF16)
    loads[1].wait()
    pooled[me, :, 256:512] = (dot(ones, v[...]) / jnp.where(kind < 64, float(MIDG), float(FARG))).astype(BF16)
    pl.semaphore_wait(barrier, count)

    mail = Mail(send_sems, recv_sems)
    ahead, back = at.next_plane(1), at.next_plane(-1)

    def relay(source, slot, place):
        target = last.at[place] if slot == 0 else win.at[slot, place]
        return mail.send(source, target, ahead)

    def share(slot, place):
        part = last.at[place] if slot == 0 else win.at[slot, place]
        return mail.send(part, part, at.core)

    hop_a1 = relay(pooled.at[me, 0:64, :], 2, me)
    far = mail.send(pooled.at[me], pooled.at[me], at.far)
    beside_a = mail.send(pooled.at[me], pooled.at[me], at.core)
    loads[2].wait()
    loads[3].wait()
    to_g = mail.send(g, go, at.head)
    to_k = mail.send(k.at[256:512, :], rim.at[:, 0:256], at.next_shard(1))
    to_v = mail.send(v.at[256:512, :], rim.at[:, 256:512], at.next_shard(1))
    to_wo = mail.send(w.at[:, lanes(1 - h)], wo, at.head)

    lane = lax.broadcasted_iota(jnp.int32, (16, 128), 1)

    def tile(bias0, bias1):
        return jnp.where(lane == 0, bias0, jnp.where(lane == 1, bias1, 0.0)).astype(BF16)

    def shut(seen):
        return jnp.where(seen, 0.0, NEG).astype(F32)

    def put(ci, at_row, value):
        for r in range(2):
            kaug[r, ci, at_row:at_row + value.shape[0], 128:256] = value

    first = tile(shut((frame_ref[0] == 1) & (p > 0)), jnp.float32(0.0))
    second = tile(jnp.float32(0.0), shut(frame_ref[1] == 1))
    for t in range(16):
        put(0, 16 * t, first)
        put(1, 16 * t, second)
    put(2, 0, jnp.zeros((256, 128), BF16))
    for slot in range(3):
        for n in range(4):
            j = 2 * (n % 2) + n // 2
            index = lax.rem(4 * slot + j - shard + 12, 12)
            real = p - 12 + index >= 0
            for r in range(4):
                keep0 = (keep_ref[0, 4 * index + r] == 1) & real
                keep1 = (keep_ref[1, 4 * index + r] == 1) & real
                if r >= 2:
                    keep0 = keep0 & (index < 11)
                put(3 + slot, 64 * n + 16 * r, tile(shut(keep0), shut(keep1)))
    rows = lax.broadcasted_iota(jnp.int32, (256, 128), 0)
    columns = lax.broadcasted_iota(jnp.int32, (256, 128), 1)
    for half in range(2):
        limit = 4 * p - 2 - 256 * half + 2 * columns
        put(6 + half, 0, jnp.where((columns < 2) & (rows >= limit), NEG, 0.0).astype(BF16))

    sub = lax.broadcasted_iota(jnp.int32, (128, 256), 0)
    subq = lax.broadcasted_iota(jnp.int32, (128, 512), 0)
    zero = jnp.zeros((), BF16)

    def by_head(source, b, r, transposed, plain):
        value = source[256 * b:256 * b + 256, 128 * r:128 * r + 128]
        turned = value.T
        for head in range(2):
            rest = slice(256 * head, 256 * head + 256)
            transposed[b, r, 0:128, rest] = jnp.where(sub // 64 == head, turned, zero)
            plain[b, r, rest, :] = jnp.where(columns // 64 == head, value, zero)

    loads[4].wait()
    q[...] = q[...] * jnp.asarray(0.125, BF16)
    for b in range(2):
        for r in range(2):
            by_head(q, b, r, qaugT, qm)
            qaugT[b, r, 128:256, :] = jnp.where(subq == b, 1.0, 0.0).astype(BF16)
            tops[b, r] = jnp.full((8, 512), NEG, F32)

    def prepare(ci):
        for r in range(2):
            lo, hi = slice(128 * r, 128 * r + 128), slice(256 + 128 * r, 384 + 128 * r)
            if ci == 0:
                kk, vv = rim[:, lo], rim[:, hi]
            elif ci < 3:
                kk, vv = k[256 * (ci - 1):256 * ci, lo], v[256 * (ci - 1):256 * ci, lo]
            elif ci < 6:
                kk, vv = win[ci - 3, :, :, lo].reshape(256, 128), win[ci - 3, :, :, hi].reshape(256, 128)
            else:
                part = slice(16 * (ci - 6), 16 * (ci - 5))
                kk, vv = coarse[part, :, lo].reshape(256, 128), coarse[part, :, hi].reshape(256, 128)
            kaug[r, ci, :, 0:128] = kk
            vcat[r, ci] = vv
            kt[r, ci] = kk.T
            vt[r, ci] = vv.T

    causal = lax.broadcasted_iota(jnp.int32, (256, 512), 0) <= lax.broadcasted_iota(jnp.int32, (256, 512), 1) % 256

    def uses(ci):
        for b in range(2):
            if ci > 2:
                yield b, ci - 1
            elif 0 <= ci - b < 2:
                yield b, ci - b

    def score(ci):
        prepare(ci)
        for r in range(2):
            for b, n in uses(ci):
                value = dot(kaug[r, ci], qaugT[b, r])
                if n == 1:
                    value = jnp.where(causal, value, NEG)
                sbuf[b, r, n] = value
                tops[b, r] = jnp.maximum(tops[b, r], fold(value, jnp.max))

    def grade(ci):
        for r in range(2):
            for b, n in uses(ci):
                dbuf[b, r, n] = dot(vcat[r, ci], gT[b, r])

    score(1)
    score(2)
    far.wait_recv()
    hop_b1 = relay(pooled.at[peer, 0:64, :], 2, peer)
    beside_b = mail.send(pooled.at[peer], pooled.at[peer], at.core)
    hop_a1.wait_recv()
    hop_a2 = relay(win.at[2, me], 1, me)
    share_a1 = share(2, me)
    beside_a.wait_recv()
    beside_b.wait_recv()
    half = lanes(c)
    total = up(pooled[0, 64:80, half])
    for n in range(1, 4):
        total = total + up(pooled[n, 64:80, half])
    coarse[at.plane, :, half] = total.astype(BF16)
    mine = coarse.at[at.plane, :, half]
    over_z = [mail.send(mine, mine, {"z": at.along_z(i)}) for i in range(1, 8)]
    hop_b1.wait_recv()
    hop_b2 = relay(win.at[2, peer], 1, peer)
    share_b1 = share(2, peer)
    hop_a2.wait_recv()
    hop_a3 = relay(win.at[1, me], 0, me)
    share_a2 = share(1, me)
    for copy in over_z:
        copy.wait_recv()
    line = coarse.at[pl.ds(8 * x, 8), :, half]
    over_x = [mail.send(line, line, {"x": at.along_x(i)}) for i in range(1, 4)]
    to_k.wait_recv()
    to_v.wait_recv()
    score(0)
    hop_b2.wait_recv()
    hop_b3 = relay(win.at[1, peer], 0, peer)
    share_b2 = share(1, peer)
    share_a1.wait_recv()
    share_b1.wait_recv()
    score(5)
    for copy in over_x:
        copy.wait_recv()
    whole = coarse.at[:, :, half]
    share_coarse = mail.send(whole, whole, at.core)
    hop_a3.wait_recv()
    share_a3 = share(0, me)
    to_g.wait_recv()
    mixed[...] = (dot_nt(g[...], w[:, lanes(h)]) + dot_nt(go[...], w[:, lanes(1 - h)])).astype(BF16)
    for b in range(2):
        for r in range(2):
            by_head(mixed, b, r, gT, gm)
    hop_b3.wait_recv()
    share_b3 = share(0, peer)
    grade(1)
    grade(2)
    share_a2.wait_recv()
    share_b2.wait_recv()
    score(4)
    share_coarse.wait_recv()
    score(6)
    score(7)
    share_a3.wait_recv()
    share_b3.wait_recv()
    for n in range(4):
        win[0, n] = jnp.where(2 * (n % 2) + n // 2 >= shard, last[n], pooled[n, 0:64, :])
    score(3)
    for ci in (0, 5, 4, 6, 7, 3):
        grade(ci)

    for r in range(2):
        for b in range(2):
            top = jnp.max(tops[b, r], axis=0, keepdims=True)
            total = jnp.zeros((8, 512), F32)
            centre = jnp.zeros((8, 512), F32)
            for n in range(7):
                e = jnp.exp(sbuf[b, r, n] - top)
                sbuf[b, r, n] = e
                total = total + fold(e, jnp.sum)
                centre = centre + fold(e * dbuf[b, r, n], jnp.sum)
            inv = 1.0 / jnp.sum(total, axis=0, keepdims=True)
            stats[b, r, 0:1] = inv
            stats[b, r, 1:2] = jnp.sum(centre, axis=0, keepdims=True) * inv
            mix = [jnp.zeros((64, 256), F32)] * 2
            for n in range(7):
                ci = n + 1 if n >= 2 else n + b
                pr = (sbuf[b, r, n] * inv).astype(BF16)
                pbuf[b, r, n] = pr
                for head in range(2):
                    mix[head] = mix[head] + dot(vt[r, ci, 64 * head:64 * head + 64, :], pr[:, 256 * head:256 * head + 256])
            for head in range(2):
                attT[r, 64 * head:64 * head + 64, 256 * b:256 * b + 256] = mix[head].astype(BF16)
        att[:, 128 * r:128 * r + 128] = attT[r].T
    to_att = mail.send(att, atto, at.head)
    turned = attT[...].reshape(256, 512)
    wg[:, lanes(h)] = dot(turned, g[...]) * (1.0 / 256.0)
    wg[:, lanes(1 - h)] = dot(turned, go[...]) * (1.0 / 256.0)
    wgb[...] = wg[pl.ds(pl.multiple_of(128 * (1 - c), 128), 128), :].astype(BF16)
    to_w = mail.send(wgb, wgr, at.core)
    for b in range(2):
        for r in range(2):
            dqT[b, r] = jnp.zeros((128, 256), F32)

    def gradients(r, ci):
        dk, dv = None, None
        for b, n in uses(ci):
            inv, centre = stats[b, r, 0:1], stats[b, r, 1:2]
            ds = (sbuf[b, r, n] * inv * (dbuf[b, r, n] - centre)).astype(BF16)
            for head in range(2):
                some = slice(64 * head, 64 * head + 64)
                dqT[b, r, some, :] += dot(kt[r, ci, some, :], ds[:, 256 * head:256 * head + 256])
            one, two = dot(ds, qm[b, r]), dot(pbuf[b, r, n], gm[b, r])
            dk, dv = (one, two) if dk is None else (dk + one, dv + two)
        for cols, value in ((slice(0, 128), dk), (slice(128, 256), dv)):
            if ci == 0:
                rimg[r, :, cols] = value.astype(BF16)
            elif ci < 3:
                near[r, 256 * (ci - 1):256 * ci, cols] = value
            elif ci < 6:
                wing[r, ci - 3, :, :, cols] = value.astype(BF16).reshape(4, 64, 128)
            else:
                cg[r, 16 * (ci - 6):16 * (ci - 5), :, cols] = value.astype(BF16).reshape(16, 16, 128)

    def finish_queries(r):
        for b in range(2):
            dq_ref[256 * b:256 * b + 256, 128 * r:128 * r + 128] = (dqT[b, r] * 0.125).astype(BF16).T

    def send_window(r):
        return mail.send(wing.at[r, :, pl.ds(2 * (1 - c), 2)], winr.at[r], at.core)

    def start_chain(r):
        beside = 2 * yh + 1 - c
        for n in range(2):
            j = 2 * n + c
            own, got = up(wing[r, 0, 2 * c + n]), up(winr[r, 0, n])
            hops[r, 0, n] = (jnp.where(j >= shard, own, 0.0) + jnp.where(j >= beside, got, 0.0)).astype(BF16)
            acc[r, 2, n] = jnp.where(j >= shard, 0.0, own) + jnp.where(j >= beside, 0.0, got)
        copy = mail.send(hops.at[r, 0], hopr.at[r, 0], back)
        for m in range(2):
            acc[r, m] = up(wing[r, 1 + m, pl.ds(2 * c, 2)]) + up(winr[r, 1 + m])
        return copy

    def go_on(r, m):
        hops[r, m] = (up(hopr[r, m - 1]) + acc[r, m - 1]).astype(BF16)
        return mail.send(hops.at[r, m], hopr.at[r, m], back)

    def end_chain(r):
        mid[r] = up(hopr[r, 2]) + acc[r, 2]
        midb[r] = mid[r, 1 - yh].astype(BF16)
        return mail.send(midb.at[r], midr.at[r], at.far)

    for ci in (3, 4, 5):
        gradients(0, ci)
    to_win0 = send_window(0)
    to_w.wait_recv()
    wx[...] = (wg[pl.ds(pl.multiple_of(128 * c, 128), 128), :] + up(wgr[...])).reshape(4, 32, 512)
    to_wx = [mail.send(wx.at[at.along_x(i)], wxr.at[i - 1], {"x": at.along_x(i)}) for i in range(1, 4)]
    gradients(0, 0)
    to_rim0 = mail.send(rimg.at[0], rimr.at[0], at.next_shard(-1))
    gradients(0, 6)
    gradients(0, 7)
    to_win0.wait_recv()
    hop_01 = start_chain(0)
    gradients(1, 6)
    gradients(1, 7)
    to_c = mail.send(cg.at[:, :, :, lanes(1 - c, 128)], cr, at.core)
    for copy in to_wx:
        copy.wait_recv()
    total = wx[x]
    for i in range(3):
        total = total + wxr[i]
    for n in range(8):
        wz[n] = total[16 * (n // 4):16 * (n // 4) + 16, 128 * (n % 4):128 * (n % 4) + 128]
    wzr[z, yh] = wz[z]
    to_wz = [mail.send(wz.at[at.along_z(i)], wzr.at[z, yh], {"z": at.along_z(i), "yh": yh if n == 0 else 1 - yh})
             for i in range(8) for n in range(2) if i + n > 0]
    gradients(1, 3)
    hop_01.wait_recv()
    hop_02 = go_on(0, 1)
    gradients(1, 4)
    gradients(1, 5)
    to_win1 = send_window(1)
    to_c.wait_recv()
    cx[...] = (up(cg[:, :, :, lanes(c, 128)]) + up(cr[...])).astype(BF16)
    to_cx = [mail.send(cx.at[:, pl.ds(8 * at.along_x(i), 8)], cxr.at[i - 1], {"x": at.along_x(i)}) for i in range(1, 4)]
    gradients(1, 0)
    to_rim1 = mail.send(rimg.at[1], rimr.at[1], at.next_shard(-1))
    to_win1.wait_recv()
    hop_11 = start_chain(1)
    hop_02.wait_recv()
    hop_03 = go_on(0, 2)
    gradients(0, 1)
    for copy in to_wz:
        copy.wait_recv()
    total = wzr[0, 0]
    for n in range(1, 16):
        total = total + wzr[n // 2, n % 2]
    wall[z] = total
    to_wall = [mail.send(wall.at[z], wall.at[z], {"z": at.along_z(i)}) for i in range(1, 8)]
    gradients(0, 2)
    finish_queries(0)
    for copy in to_cx:
        copy.wait_recv()
    total = up(cx[:, pl.ds(8 * x, 8)])
    for i in range(3):
        total = total + up(cxr[i])
    cz[...] = total.astype(BF16)
    to_cz = [mail.send(cz.at[:, at.along_z(i)], czr.at[i - 1], {"z": at.along_z(i)}) for i in range(1, 8)]
    hop_11.wait_recv()
    hop_12 = go_on(1, 1)
    hop_03.wait_recv()
    to_mid0 = end_chain(0)
    gradients(1, 1)
    for copy in to_wall:
        copy.wait_recv()
    for n in range(8):
        weight_ref[c, x, 16 * (n // 4):16 * (n // 4) + 16, 128 * (n % 4):128 * (n % 4) + 128] = wall[n]
    line = weight_ref.at[c, x]
    to_line = [mail.send(line, line, {"x": at.along_x(i)}) for i in range(1, 4)]
    gradients(1, 2)
    finish_queries(1)
    hop_12.wait_recv()
    hop_13 = go_on(1, 2)
    for copy in to_cz:
        copy.wait_recv()
    total = up(cz[:, z])
    for i in range(7):
        total = total + up(czr[i])
    cp[...] = total.astype(BF16)
    to_cp = [mail.send(cp, cpr.at[n], who) for n, who in enumerate((at.far, at.core, at.diagonal))]
    to_att.wait_recv()
    to_wo.wait_recv()
    out_ref[...] = (dot(att[...], w[:, lanes(h)]) + dot(atto[...], wo[...])).astype(BF16)
    for copy in to_line:
        copy.wait_recv()
    to_half = mail.send(weight_ref.at[c], weight_ref.at[c], at.core)
    hop_13.wait_recv()
    to_mid1 = end_chain(1)
    for copy in to_cp:
        copy.wait_recv()
    for r in range(2):
        cfull[r, :, lanes(c, 128)] = up(cp[r]) + up(cpr[0, r])
        cfull[r, :, lanes(1 - c, 128)] = up(cpr[1, r]) + up(cpr[2, r])
    token = lax.broadcasted_iota(jnp.int32, (512, 80), 0)
    row = lax.broadcasted_iota(jnp.int32, (512, 80), 1)
    spread = jnp.where(jnp.where(row < 64, token // MIDG, 64 + 4 * shard + token // FARG) == row, 1.0, 0.0).astype(BF16)
    row = lax.broadcasted_iota(jnp.int32, (80, 256), 0)
    value_lane = lax.broadcasted_iota(jnp.int32, (80, 256), 1) >= 128
    divisor = jnp.where(row < 64, jnp.where(value_lane, float(MIDG), math.sqrt(MIDG)), jnp.where(value_lane, float(FARG), math.sqrt(FARG)))
    for r, to_mid, to_rim in ((0, to_mid0, to_rim0), (1, to_mid1, to_rim1)):
        to_rim.wait_recv()
        to_mid.wait_recv()
        pools = jnp.concatenate([mid[r, yh] + up(midr[r]), cfull[r]], axis=0) / divisor
        high = pools.astype(BF16)
        low = (pools - up(high)).astype(BF16)
        added = dot(spread, high) + dot(spread, low) + near[r]
        for target, cols in ((kg_ref, slice(0, 128)), (vg_ref, slice(128, 256))):
            target[0:256, 128 * r:128 * r + 128] = added[0:256, cols].astype(BF16)
            target[256:512, 128 * r:128 * r + 128] = (added[256:512, cols] + up(rimr[r, :, cols])).astype(BF16)
    to_half.wait_recv()
    mail.finish()


def on_device(queries, key_vectors, value_vectors, out_grad, out_weight, mid_keep, frame_keep):
    B, S = (lambda *s: pltpu.VMEM(s, BF16)), (lambda *s: pltpu.VMEM(s, F32))
    T = jax.ShapeDtypeStruct((512, 256), BF16)
    output, dq, kg, vg, weight = pl.pallas_call(
        layer_kernel,
        out_shape=[T, T, T, T, jax.ShapeDtypeStruct((2, 4, 32, 512), F32)],
        in_specs=[ANY] * 5 + [SM] * 2,
        out_specs=[VM] * 5,
        scratch_shapes=[
            B(512, 256), B(512, 256), B(512, 256), B(512, 256), B(256, 512), B(256, 512), B(512, 256), B(256, 256),
            B(4, 80, 512), B(3, 4, 64, 512), B(4, 64, 512), B(32, 16, 512), B(512, 256),
            B(2, 8, 256, 256), B(2, 8, 256, 128), B(2, 8, 128, 256), B(2, 8, 128, 256),
            B(2, 2, 256, 512), B(2, 2, 128, 512), B(2, 2, 512, 128), B(2, 2, 512, 128),
            S(2, 2, 7, 256, 512), S(2, 2, 7, 256, 512), B(2, 2, 7, 256, 512), S(2, 2, 8, 512), S(2, 2, 8, 512),
            B(2, 128, 512), B(512, 256), B(512, 256), S(2, 2, 128, 256), S(256, 512), B(128, 512), B(128, 512),
            S(4, 32, 512), S(3, 32, 512), S(8, 16, 128), S(8, 2, 16, 128), S(8, 16, 128),
            S(2, 512, 256), B(2, 256, 256), B(2, 256, 256), B(2, 3, 4, 64, 256), B(2, 3, 2, 64, 256),
            S(2, 3, 2, 64, 256), B(2, 3, 2, 64, 256), B(2, 3, 2, 64, 256), S(2, 2, 64, 256), B(2, 64, 256), B(2, 64, 256),
            B(2, 32, 16, 256), B(2, 32, 16, 128), B(2, 32, 16, 128), B(3, 2, 8, 16, 128), B(2, 8, 16, 128),
            B(7, 2, 16, 128), B(2, 16, 128), B(3, 2, 16, 128), S(2, 16, 256),
            pltpu.SemaphoreType.DMA((5,)), pltpu.SemaphoreType.DMA((90,)), pltpu.SemaphoreType.DMA((90,))],
        compiler_params=pltpu.CompilerParams(collective_id=0, has_side_effects=True, vmem_limit_bytes=60 * 2**20),
        name="layer",
    )(queries, key_vectors, value_vectors, out_grad, out_weight, mid_keep, frame_keep)
    return output, dq, kg, vg, weight.reshape(256, 512)


def solution(mesh):
    split = Mesh(mesh.devices.reshape(4, 8, 2, 2, 2), ("x", "z", "yh", "c", "h"))
    seq = ("x", "z", "yh", "c")
    return jax.shard_map(
        on_device,
        mesh=split,
        in_specs=(P(seq, "h"), P(seq, "h"), P(seq, "h"), P(seq, "h"), P("h", None), P(seq, None), P(seq)),
        out_specs=(P(seq, "h"), P(seq, "h"), P(seq, "h"), P(seq, "h"), P("h", None)),
        check_vma=False,
    )
```

time: 98.6 us -> 76 us (0.77)
  the two profiles are of different devices: /device:TPU:1 before, /device:TPU:16 now
where the time goes in v2:
time: 76 us; the launch traced here: 75.8 us
  Pallas kernels  70.2 us (92%)
  local copies, waits for them, and re-layouts  4.96 us (7%)
    pallas_call x1, Pallas kernels, on_device(): pl.pallas_call(layer_kernel, out_shape=[T, T, T, T, jax.ShapeDtypeStruct(...  70.2 us
    unnamed x13, local copies, waits for them, and re-layouts  4.96 us

profile of v2, /device:TPU:16, one launch (start us, length us, event | category | flops | bytes accessed | tf_op | source)
XLA Modules:
  0.0 75.8 jit_solution(4073990628074363820)
XLA Ops:
  0.6 70.2 %layer.1 = (bf16[512,256]{1,0:T(8,128)(2,1)}, bf16[512,256]{1,0:T(8,128)(2,1)}, bf16[512,256]{1,0:T(8,128)(2,1)}, bf16[512,256]{1,0:T(8,128)(2,1)}, f32[2,4,32,512]{3,2,1,0:T(8,128)}) custom-call(bf16[512,256]{1,0:T(8,128)(2,1)} %q_hbm.1, bf16[512,256]{1,0:T(8,128)(2,1)} %k_hbm.1, bf16[512,256]{1,0:T(8,128)(2,1)} %v_hbm.1, bf16[512,256]{1,0:T(8,128)(2,1)} %g_hbm.1, ...), custom_call_target="tpu_custom_call" | custom-call | tf_op jit(solution)/shard_map/layer/pallas_call | solution.py:506
  70.9 0.0 copy-start.3
  70.9 1.7 %copy.17 = bf16[512,256]{1,0:T(8,128)(2,1)} copy(bf16[512,256]{1,0:T(8,128)(2,1)} %get-tuple-element.20) | data formatting | bytes 524288
  72.6 0.0 copy-done.3
  72.6 0.0 copy-start.2
  72.6 0.0 copy-start.1
  72.6 0.7 copy.18
  73.3 0.3 copy-done.2
  73.6 0.0 copy-start
  73.6 0.7 copy.19
  74.3 0.0 copy-done.1
  74.3 0.7 copy.20
  75.0 0.0 copy-done
  75.0 0.8 %copy.21 = f32[256,512]{1,0:T(8,128)} copy(f32[256,512]{1,0:T(8,128)S(1)} %bitcast.1) | data formatting | bytes 1048576
Async XLA Ops:
  70.9 1.7 %copy-start.3 = (bf16[512,256]{1,0:T(8,128)(2,1)S(1)}, bf16[512,256]{1,0:T(8,128)(2,1)}, u32[]{:S(2)}) copy-start(bf16[512,256]{1,0:T(8,128)(2,1)} %get-tuple-element.21) | copy-start | bytes 786436
  72.6 1.0 %copy-start.2 = (bf16[512,256]{1,0:T(8,128)(2,1)S(1)}, bf16[512,256]{1,0:T(8,128)(2,1)}, u32[]{:S(2)}) copy-start(bf16[512,256]{1,0:T(8,128)(2,1)} %get-tuple-element.22) | copy-start | bytes 786436
  72.6 1.8 %copy-start.1 = (bf16[512,256]{1,0:T(8,128)(2,1)S(1)}, bf16[512,256]{1,0:T(8,128)(2,1)}, u32[]{:S(2)}) copy-start(bf16[512,256]{1,0:T(8,128)(2,1)} %get-tuple-element.23) | copy-start | bytes 786436
  73.6 1.4 %copy-start = (f32[2,4,32,512]{3,2,1,0:T(8,128)S(1)}, f32[2,4,32,512]{3,2,1,0:T(8,128)}, u32[]{:S(2)}) copy-start(f32[2,4,32,512]{3,2,1,0:T(8,128)} %get-tuple-element.14) | copy-start | bytes 1572868

commit v3 on v2

--- a/solution.py
+++ b/solution.py
@@ -62,9 +62,10 @@
         return {"x": to // 32, "z": lax.rem(to // 4, 8), "yh": lax.rem(to // 2, 2), "c": lax.rem(to, 2)}
 
     def greet(self, diagonal):
-        peers = [self.core, self.far, self.head, self.next_plane(1), self.next_plane(-1), self.next_shard(1), self.next_shard(-1)]
+        peers = [self.core, self.far, self.head, *[self.next_plane(d) for d in (1, 2, 3, -1, -2, -3)], self.next_shard(1), self.next_shard(-1)]
         peers += [{"z": self.along_z(i)} for i in range(1, 8)]
         peers += [{"x": self.along_x(i)} for i in range(1, 4)]
+        peers += [{"x": self.along_x(i), "yh": 1 - self.yh} for i in range(1, 4)]
         if diagonal:
             peers.append(self.diagonal)
         barrier = pltpu.get_barrier_semaphore()
@@ -93,21 +94,28 @@
 
 
 def layer_kernel(q_hbm, k_hbm, v_hbm, g_hbm, w_hbm, keep_ref, frame_ref,
+                 out_hbm, dq_hbm, kg_hbm, vg_hbm, weight_hbm,
                  out_ref, dq_ref, kg_ref, vg_ref, weight_ref,
-                 q, k, v, g, w, rim, go, wo, pooled, win, last, coarse, mixed,
+                 q, k, v, g, w, rim, go, wo, pooled, win, last, coarse, coarse4, mixed,
                  kaug, vcat, kt, vt, qaugT, gT, qm, gm, sbuf, dbuf, pbuf, tops, stats,
                  attT, att, atto, dqT, wg, wgb, wgr, wx, wxr, wz, wzr, wall,
-                 near, rimg, rimr, wing, winr, acc, hops, hopr, mid, midb, midr,
+                 near, rimg, rimr, wing, winr, acc, fars, farr, outs, backs, lines,
                  cg, cr, cx, cxr, cz, czr, cp, cpr, cfull,
-                 load_sems, send_sems, recv_sems):
+                 load_sems, store_sems, send_sems, recv_sems):
     at = Place()
     c, x, z, yh, h, shard = at.c, at.x, at.z, at.yh, at.h, at.shard
     p = 4 * at.plane + shard
     loads = [pltpu.make_async_copy(a, b, load_sems.at[n])
              for n, (a, b) in enumerate(((k_hbm, k), (v_hbm, v), (g_hbm, g), (w_hbm, w), (q_hbm, q)))]
-    for load in loads:
+    for load in loads[:2]:
         load.start()
     barrier, count = at.greet(True)
+    stores = []
+
+    def store(n, source, target):
+        copy = pltpu.make_async_copy(source, target, store_sems.at[n])
+        copy.start()
+        stores.append(copy)
 
     def lanes(n, size=256):
         return pl.ds(pl.multiple_of(size * n, size), size)
@@ -120,13 +128,19 @@
     kind = lax.broadcasted_iota(jnp.int32, (80, 256), 0)
     me, peer = 2 * c + yh, 2 * c + 1 - yh
     loads[0].wait()
-    pooled[me, :, 0:256] = (dot(ones, k[...]) / jnp.where(kind < 64, math.sqrt(MIDG), math.sqrt(FARG))).astype(BF16)
+    keys = (dot(ones, k[...]) / jnp.where(kind < 64, math.sqrt(MIDG), math.sqrt(FARG))).astype(BF16)
+    pooled[me, :, 0:256] = keys[0:64]
+    coarse4[me, :, 0:256] = keys[64:80]
     loads[1].wait()
-    pooled[me, :, 256:512] = (dot(ones, v[...]) / jnp.where(kind < 64, float(MIDG), float(FARG))).astype(BF16)
+    values = (dot(ones, v[...]) / jnp.where(kind < 64, float(MIDG), float(FARG))).astype(BF16)
+    pooled[me, :, 256:512] = values[0:64]
+    coarse4[me, :, 256:512] = values[64:80]
+    for load in loads[2:]:
+        load.start()
     pl.semaphore_wait(barrier, count)
 
     mail = Mail(send_sems, recv_sems)
-    ahead, back = at.next_plane(1), at.next_plane(-1)
+    ahead = at.next_plane(1)
 
     def relay(source, slot, place):
         target = last.at[place] if slot == 0 else win.at[slot, place]
@@ -136,15 +150,10 @@
         part = last.at[place] if slot == 0 else win.at[slot, place]
         return mail.send(part, part, at.core)
 
-    hop_a1 = relay(pooled.at[me, 0:64, :], 2, me)
+    over_plane = [mail.send(coarse4.at[me], coarse4.at[me], who) for who in (at.diagonal, at.far, at.core)]
     far = mail.send(pooled.at[me], pooled.at[me], at.far)
+    hop_a1 = relay(pooled.at[me], 2, me)
     beside_a = mail.send(pooled.at[me], pooled.at[me], at.core)
-    loads[2].wait()
-    loads[3].wait()
-    to_g = mail.send(g, go, at.head)
-    to_k = mail.send(k.at[256:512, :], rim.at[:, 0:256], at.next_shard(1))
-    to_v = mail.send(v.at[256:512, :], rim.at[:, 256:512], at.next_shard(1))
-    to_wo = mail.send(w.at[:, lanes(1 - h)], wo, at.head)
 
     lane = lax.broadcasted_iota(jnp.int32, (16, 128), 1)
 
@@ -237,89 +246,84 @@
                 sbuf[b, r, n] = value
                 tops[b, r] = jnp.maximum(tops[b, r], fold(value, jnp.max))
 
-    def grade(ci):
-        for r in range(2):
-            for b, n in uses(ci):
-                dbuf[b, r, n] = dot(vcat[r, ci], gT[b, r])
-
-    score(1)
-    score(2)
-    far.wait_recv()
-    hop_b1 = relay(pooled.at[peer, 0:64, :], 2, peer)
-    beside_b = mail.send(pooled.at[peer], pooled.at[peer], at.core)
+    half = lanes(c)
+    for copy in over_plane:
+        copy.wait_recv()
+    total = up(coarse4[0, :, half])
+    for n in range(1, 4):
+        total = total + up(coarse4[n, :, half])
+    coarse[at.plane, :, half] = total.astype(BF16)
+    mine = coarse.at[at.plane, :, half]
+    over_z = [mail.send(mine, mine, {"z": at.along_z(i)}) for i in range(1, 8)]
     hop_a1.wait_recv()
     hop_a2 = relay(win.at[2, me], 1, me)
     share_a1 = share(2, me)
-    beside_a.wait_recv()
-    beside_b.wait_recv()
-    half = lanes(c)
-    total = up(pooled[0, 64:80, half])
-    for n in range(1, 4):
-        total = total + up(pooled[n, 64:80, half])
-    coarse[at.plane, :, half] = total.astype(BF16)
-    mine = coarse.at[at.plane, :, half]
-    over_z = [mail.send(mine, mine, {"z": at.along_z(i)}) for i in range(1, 8)]
+    far.wait_recv()
+    hop_b1 = relay(pooled.at[peer], 2, peer)
+    beside_b = mail.send(pooled.at[peer], pooled.at[peer], at.core)
+    loads[2].wait()
+    to_g = mail.send(g, go, at.head)
+    to_k = mail.send(k.at[256:512, :], rim.at[:, 0:256], at.next_shard(1))
+    to_v = mail.send(v.at[256:512, :], rim.at[:, 256:512], at.next_shard(1))
+    score(1)
+    hop_a2.wait_recv()
+    hop_a3 = relay(win.at[1, me], 0, me)
+    share_a2 = share(1, me)
     hop_b1.wait_recv()
     hop_b2 = relay(win.at[2, peer], 1, peer)
     share_b1 = share(2, peer)
-    hop_a2.wait_recv()
-    hop_a3 = relay(win.at[1, me], 0, me)
-    share_a2 = share(1, me)
+    score(2)
     for copy in over_z:
         copy.wait_recv()
     line = coarse.at[pl.ds(8 * x, 8), :, half]
     over_x = [mail.send(line, line, {"x": at.along_x(i)}) for i in range(1, 4)]
+    share_a1.wait_recv()
+    share_b1.wait_recv()
+    hop_a3.wait_recv()
+    share_a3 = share(0, me)
+    hop_b2.wait_recv()
+    hop_b3 = relay(win.at[1, peer], 0, peer)
+    share_b2 = share(1, peer)
+    score(5)
     to_k.wait_recv()
     to_v.wait_recv()
     score(0)
-    hop_b2.wait_recv()
-    hop_b3 = relay(win.at[1, peer], 0, peer)
-    share_b2 = share(1, peer)
-    share_a1.wait_recv()
-    share_b1.wait_recv()
-    score(5)
+    share_a2.wait_recv()
+    share_b2.wait_recv()
+    score(4)
+    hop_b3.wait_recv()
+    share_b3 = share(0, peer)
     for copy in over_x:
         copy.wait_recv()
     whole = coarse.at[:, :, half]
     share_coarse = mail.send(whole, whole, at.core)
-    hop_a3.wait_recv()
-    share_a3 = share(0, me)
+    loads[3].wait()
     to_g.wait_recv()
     mixed[...] = (dot_nt(g[...], w[:, lanes(h)]) + dot_nt(go[...], w[:, lanes(1 - h)])).astype(BF16)
     for b in range(2):
         for r in range(2):
             by_head(mixed, b, r, gT, gm)
-    hop_b3.wait_recv()
-    share_b3 = share(0, peer)
-    grade(1)
-    grade(2)
-    share_a2.wait_recv()
-    share_b2.wait_recv()
-    score(4)
+    share_a3.wait_recv()
+    share_b3.wait_recv()
+    beside_a.wait_recv()
+    beside_b.wait_recv()
+    for n in range(4):
+        win[0, n] = jnp.where(2 * (n % 2) + n // 2 >= shard, last[n], pooled[n])
+    score(3)
     share_coarse.wait_recv()
     score(6)
     score(7)
-    share_a3.wait_recv()
-    share_b3.wait_recv()
-    for n in range(4):
-        win[0, n] = jnp.where(2 * (n % 2) + n // 2 >= shard, last[n], pooled[n, 0:64, :])
-    score(3)
-    for ci in (0, 5, 4, 6, 7, 3):
-        grade(ci)
 
     for r in range(2):
         for b in range(2):
             top = jnp.max(tops[b, r], axis=0, keepdims=True)
             total = jnp.zeros((8, 512), F32)
-            centre = jnp.zeros((8, 512), F32)
             for n in range(7):
                 e = jnp.exp(sbuf[b, r, n] - top)
                 sbuf[b, r, n] = e
                 total = total + fold(e, jnp.sum)
-                centre = centre + fold(e * dbuf[b, r, n], jnp.sum)
             inv = 1.0 / jnp.sum(total, axis=0, keepdims=True)
             stats[b, r, 0:1] = inv
-            stats[b, r, 1:2] = jnp.sum(centre, axis=0, keepdims=True) * inv
             mix = [jnp.zeros((64, 256), F32)] * 2
             for n in range(7):
                 ci = n + 1 if n >= 2 else n + b
@@ -330,15 +334,26 @@
             for head in range(2):
                 attT[r, 64 * head:64 * head + 64, 256 * b:256 * b + 256] = mix[head].astype(BF16)
         att[:, 128 * r:128 * r + 128] = attT[r].T
-    to_att = mail.send(att, atto, at.head)
     turned = attT[...].reshape(256, 512)
     wg[:, lanes(h)] = dot(turned, g[...]) * (1.0 / 256.0)
     wg[:, lanes(1 - h)] = dot(turned, go[...]) * (1.0 / 256.0)
     wgb[...] = wg[pl.ds(pl.multiple_of(128 * (1 - c), 128), 128), :].astype(BF16)
     to_w = mail.send(wgb, wgr, at.core)
+    to_att = mail.send(att, atto, at.head)
+    to_wo = mail.send(w.at[:, lanes(1 - h)], wo, at.head)
     for b in range(2):
         for r in range(2):
             dqT[b, r] = jnp.zeros((128, 256), F32)
+
+    def grade(r):
+        for b in range(2):
+            centre = jnp.zeros((8, 512), F32)
+            for n in range(7):
+                ci = n + 1 if n >= 2 else n + b
+                graded = dot(vcat[r, ci], gT[b, r])
+                dbuf[b, r, n] = graded
+                centre = centre + fold(sbuf[b, r, n] * graded, jnp.sum)
+            stats[b, r, 1:2] = jnp.sum(centre, axis=0, keepdims=True) * stats[b, r, 0:1]
 
     def gradients(r, ci):
         dk, dv = None, None
@@ -367,68 +382,57 @@
     def send_window(r):
         return mail.send(wing.at[r, :, pl.ds(2 * (1 - c), 2)], winr.at[r], at.core)
 
-    def start_chain(r):
+    def to_far_plane(r):
         beside = 2 * yh + 1 - c
         for n in range(2):
             j = 2 * n + c
             own, got = up(wing[r, 0, 2 * c + n]), up(winr[r, 0, n])
-            hops[r, 0, n] = (jnp.where(j >= shard, own, 0.0) + jnp.where(j >= beside, got, 0.0)).astype(BF16)
-            acc[r, 2, n] = jnp.where(j >= shard, 0.0, own) + jnp.where(j >= beside, 0.0, got)
-        copy = mail.send(hops.at[r, 0], hopr.at[r, 0], back)
-        for m in range(2):
-            acc[r, m] = up(wing[r, 1 + m, pl.ds(2 * c, 2)]) + up(winr[r, 1 + m])
-        return copy
-
-    def go_on(r, m):
-        hops[r, m] = (up(hopr[r, m - 1]) + acc[r, m - 1]).astype(BF16)
-        return mail.send(hops.at[r, m], hopr.at[r, m], back)
-
-    def end_chain(r):
-        mid[r] = up(hopr[r, 2]) + acc[r, 2]
-        midb[r] = mid[r, 1 - yh].astype(BF16)
-        return mail.send(midb.at[r], midr.at[r], at.far)
-
-    for ci in (3, 4, 5):
-        gradients(0, ci)
-    to_win0 = send_window(0)
+            acc[r, n, 3] = jnp.where(j >= shard, own, 0.0) + jnp.where(j >= beside, got, 0.0)
+            acc[r, n, 0] = jnp.where(j >= shard, 0.0, own) + jnp.where(j >= beside, 0.0, got)
+            for m in range(2):
+                acc[r, n, 2 - m] = up(wing[r, 1 + m, 2 * c + n]) + up(winr[r, 1 + m, n])
+        fars[r] = acc[r, 1 - yh].astype(BF16)
+        return mail.send(fars.at[r], farr.at[r], at.far)
+
+    def to_owners(r):
+        total = acc[r, yh] + up(farr[r])
+        acc[r, yh] = total
+        outs[r] = total[1:4].astype(BF16)
+        return [mail.send(outs.at[r, d - 1], backs.at[r, d - 1], at.next_plane(-d)) for d in (3, 2, 1)]
+
+    grade(0)
     to_w.wait_recv()
-    wx[...] = (wg[pl.ds(pl.multiple_of(128 * c, 128), 128), :] + up(wgr[...])).reshape(4, 32, 512)
+    wx[...] = (wg[pl.ds(pl.multiple_of(128 * c, 128), 128), :] + up(wgr[...])).astype(BF16).reshape(4, 32, 512)
     to_wx = [mail.send(wx.at[at.along_x(i)], wxr.at[i - 1], {"x": at.along_x(i)}) for i in range(1, 4)]
-    gradients(0, 0)
-    to_rim0 = mail.send(rimg.at[0], rimr.at[0], at.next_shard(-1))
     gradients(0, 6)
     gradients(0, 7)
-    to_win0.wait_recv()
-    hop_01 = start_chain(0)
+    grade(1)
     gradients(1, 6)
     gradients(1, 7)
     to_c = mail.send(cg.at[:, :, :, lanes(1 - c, 128)], cr, at.core)
     for copy in to_wx:
         copy.wait_recv()
-    total = wx[x]
+    total = up(wx[x])
     for i in range(3):
-        total = total + wxr[i]
+        total = total + up(wxr[i])
     for n in range(8):
         wz[n] = total[16 * (n // 4):16 * (n // 4) + 16, 128 * (n % 4):128 * (n % 4) + 128]
     wzr[z, yh] = wz[z]
     to_wz = [mail.send(wz.at[at.along_z(i)], wzr.at[z, yh], {"z": at.along_z(i), "yh": yh if n == 0 else 1 - yh})
              for i in range(8) for n in range(2) if i + n > 0]
-    gradients(1, 3)
-    hop_01.wait_recv()
-    hop_02 = go_on(0, 1)
-    gradients(1, 4)
-    gradients(1, 5)
-    to_win1 = send_window(1)
+    gradients(0, 3)
+    gradients(0, 4)
     to_c.wait_recv()
     cx[...] = (up(cg[:, :, :, lanes(c, 128)]) + up(cr[...])).astype(BF16)
     to_cx = [mail.send(cx.at[:, pl.ds(8 * at.along_x(i), 8)], cxr.at[i - 1], {"x": at.along_x(i)}) for i in range(1, 4)]
-    gradients(1, 0)
-    to_rim1 = mail.send(rimg.at[1], rimr.at[1], at.next_shard(-1))
-    to_win1.wait_recv()
-    hop_11 = start_chain(1)
-    hop_02.wait_recv()
-    hop_03 = go_on(0, 2)
-    gradients(0, 1)
+    gradients(0, 5)
+    to_win0 = send_window(0)
+    gradients(1, 3)
+    gradients(1, 4)
+    to_win0.wait_recv()
+    to_far0 = to_far_plane(0)
+    gradients(1, 5)
+    to_win1 = send_window(1)
     for copy in to_wz:
         copy.wait_recv()
     total = wzr[0, 0]
@@ -436,8 +440,12 @@
         total = total + wzr[n // 2, n % 2]
     wall[z] = total
     to_wall = [mail.send(wall.at[z], wall.at[z], {"z": at.along_z(i)}) for i in range(1, 8)]
-    gradients(0, 2)
-    finish_queries(0)
+    gradients(0, 0)
+    gradients(1, 0)
+    to_rim0 = mail.send(rimg.at[0], rimr.at[0], at.next_shard(-1))
+    to_rim1 = mail.send(rimg.at[1], rimr.at[1], at.next_shard(-1))
+    to_win1.wait_recv()
+    to_far1 = to_far_plane(1)
     for copy in to_cx:
         copy.wait_recv()
     total = up(cx[:, pl.ds(8 * x, 8)])
@@ -445,21 +453,27 @@
         total = total + up(cxr[i])
     cz[...] = total.astype(BF16)
     to_cz = [mail.send(cz.at[:, at.along_z(i)], czr.at[i - 1], {"z": at.along_z(i)}) for i in range(1, 8)]
-    hop_11.wait_recv()
-    hop_12 = go_on(1, 1)
-    hop_03.wait_recv()
-    to_mid0 = end_chain(0)
+    gradients(0, 1)
+    gradients(0, 2)
+    finish_queries(0)
+    to_far0.wait_recv()
+    to_own0 = to_owners(0)
     gradients(1, 1)
-    for copy in to_wall:
-        copy.wait_recv()
-    for n in range(8):
-        weight_ref[c, x, 16 * (n // 4):16 * (n // 4) + 16, 128 * (n % 4):128 * (n % 4) + 128] = wall[n]
-    line = weight_ref.at[c, x]
-    to_line = [mail.send(line, line, {"x": at.along_x(i)}) for i in range(1, 4)]
     gradients(1, 2)
     finish_queries(1)
-    hop_12.wait_recv()
-    hop_13 = go_on(1, 2)
+    store(0, dq_ref, dq_hbm)
+    for copy in to_wall:
+        copy.wait_recv()
+    for n in range(8):
+        lines[c, x, 16 * (n // 4):16 * (n // 4) + 16, 128 * (n % 4):128 * (n % 4) + 128] = wall[n].astype(BF16)
+    line = lines.at[c, x]
+    to_line = [mail.send(line, line, {"x": at.along_x(i)}) for i in range(1, 4)]
+    to_far1.wait_recv()
+    to_own1 = to_owners(1)
+    to_att.wait_recv()
+    to_wo.wait_recv()
+    out_ref[...] = (dot(att[...], w[:, lanes(h)]) + dot(atto[...], wo[...])).astype(BF16)
+    store(1, out_ref, out_hbm)
     for copy in to_cz:
         copy.wait_recv()
     total = up(cz[:, z])
@@ -467,37 +481,45 @@
         total = total + up(czr[i])
     cp[...] = total.astype(BF16)
     to_cp = [mail.send(cp, cpr.at[n], who) for n, who in enumerate((at.far, at.core, at.diagonal))]
-    to_att.wait_recv()
-    to_wo.wait_recv()
-    out_ref[...] = (dot(att[...], w[:, lanes(h)]) + dot(atto[...], wo[...])).astype(BF16)
     for copy in to_line:
         copy.wait_recv()
-    to_half = mail.send(weight_ref.at[c], weight_ref.at[c], at.core)
-    hop_13.wait_recv()
-    to_mid1 = end_chain(1)
+    to_half = mail.send(lines.at[c], lines.at[c], at.core)
     for copy in to_cp:
         copy.wait_recv()
     for r in range(2):
         cfull[r, :, lanes(c, 128)] = up(cp[r]) + up(cpr[0, r])
         cfull[r, :, lanes(1 - c, 128)] = up(cpr[1, r]) + up(cpr[2, r])
+    to_half.wait_recv()
+    weight_ref[...] = up(lines[...])
+    store(4, weight_ref, weight_hbm)
     token = lax.broadcasted_iota(jnp.int32, (512, 80), 0)
     row = lax.broadcasted_iota(jnp.int32, (512, 80), 1)
     spread = jnp.where(jnp.where(row < 64, token // MIDG, 64 + 4 * shard + token // FARG) == row, 1.0, 0.0).astype(BF16)
     row = lax.broadcasted_iota(jnp.int32, (80, 256), 0)
     value_lane = lax.broadcasted_iota(jnp.int32, (80, 256), 1) >= 128
     divisor = jnp.where(row < 64, jnp.where(value_lane, float(MIDG), math.sqrt(MIDG)), jnp.where(value_lane, float(FARG), math.sqrt(FARG)))
-    for r, to_mid, to_rim in ((0, to_mid0, to_rim0), (1, to_mid1, to_rim1)):
+    for r, to_own, to_rim in ((0, to_own0, to_rim0), (1, to_own1, to_rim1)):
         to_rim.wait_recv()
-        to_mid.wait_recv()
-        pools = jnp.concatenate([mid[r, yh] + up(midr[r]), cfull[r]], axis=0) / divisor
+        for copy in to_own:
+            copy.wait_recv()
+        middle = acc[r, yh, 0] + up(backs[r, 0]) + up(backs[r, 1]) + up(backs[r, 2])
+        pools = jnp.concatenate([middle, cfull[r]], axis=0) / divisor
         high = pools.astype(BF16)
         low = (pools - up(high)).astype(BF16)
         added = dot(spread, high) + dot(spread, low) + near[r]
         for target, cols in ((kg_ref, slice(0, 128)), (vg_ref, slice(128, 256))):
             target[0:256, 128 * r:128 * r + 128] = added[0:256, cols].astype(BF16)
             target[256:512, 128 * r:128 * r + 128] = (added[256:512, cols] + up(rimr[r, :, cols])).astype(BF16)
-    to_half.wait_recv()
+    store(2, kg_ref, kg_hbm)
+    store(3, vg_ref, vg_hbm)
+    for copy in stores:
+        copy.wait()
     mail.finish()
+
+
+def handed_on(*refs):
+    for n in range(5):
+        refs[5 + n][...] = refs[n][...]
 
 
 def on_device(queries, key_vectors, value_vectors, out_grad, out_weight, mid_keep, frame_keep):
@@ -507,23 +529,32 @@
         layer_kernel,
         out_shape=[T, T, T, T, jax.ShapeDtypeStruct((2, 4, 32, 512), F32)],
         in_specs=[ANY] * 5 + [SM] * 2,
-        out_specs=[VM] * 5,
+        out_specs=[ANY] * 5,
         scratch_shapes=[
+            B(512, 256), B(512, 256), B(512, 256), B(512, 256), S(2, 4, 32, 512),
             B(512, 256), B(512, 256), B(512, 256), B(512, 256), B(256, 512), B(256, 512), B(512, 256), B(256, 256),
-            B(4, 80, 512), B(3, 4, 64, 512), B(4, 64, 512), B(32, 16, 512), B(512, 256),
+            B(4, 64, 512), B(3, 4, 64, 512), B(4, 64, 512), B(32, 16, 512), B(4, 16, 512), B(512, 256),
             B(2, 8, 256, 256), B(2, 8, 256, 128), B(2, 8, 128, 256), B(2, 8, 128, 256),
             B(2, 2, 256, 512), B(2, 2, 128, 512), B(2, 2, 512, 128), B(2, 2, 512, 128),
             S(2, 2, 7, 256, 512), S(2, 2, 7, 256, 512), B(2, 2, 7, 256, 512), S(2, 2, 8, 512), S(2, 2, 8, 512),
             B(2, 128, 512), B(512, 256), B(512, 256), S(2, 2, 128, 256), S(256, 512), B(128, 512), B(128, 512),
-            S(4, 32, 512), S(3, 32, 512), S(8, 16, 128), S(8, 2, 16, 128), S(8, 16, 128),
+            B(4, 32, 512), B(3, 32, 512), S(8, 16, 128), S(8, 2, 16, 128), S(8, 16, 128),
             S(2, 512, 256), B(2, 256, 256), B(2, 256, 256), B(2, 3, 4, 64, 256), B(2, 3, 2, 64, 256),
-            S(2, 3, 2, 64, 256), B(2, 3, 2, 64, 256), B(2, 3, 2, 64, 256), S(2, 2, 64, 256), B(2, 64, 256), B(2, 64, 256),
+            S(2, 2, 4, 64, 256), B(2, 4, 64, 256), B(2, 4, 64, 256), B(2, 3, 64, 256), B(2, 3, 64, 256), B(2, 4, 32, 512),
             B(2, 32, 16, 256), B(2, 32, 16, 128), B(2, 32, 16, 128), B(3, 2, 8, 16, 128), B(2, 8, 16, 128),
             B(7, 2, 16, 128), B(2, 16, 128), B(3, 2, 16, 128), S(2, 16, 256),
-            pltpu.SemaphoreType.DMA((5,)), pltpu.SemaphoreType.DMA((90,)), pltpu.SemaphoreType.DMA((90,))],
+            pltpu.SemaphoreType.DMA((5,)), pltpu.SemaphoreType.DMA((5,)), pltpu.SemaphoreType.DMA((90,)), pltpu.SemaphoreType.DMA((90,))],
         compiler_params=pltpu.CompilerParams(collective_id=0, has_side_effects=True, vmem_limit_bytes=60 * 2**20),
         name="layer",
     )(queries, key_vectors, value_vectors, out_grad, out_weight, mid_keep, frame_keep)
+    shapes = [T, T, T, T, jax.ShapeDtypeStruct((2, 4, 32, 512), F32)]
+    output, dq, kg, vg, weight = pl.pallas_call(
+        handed_on,
+        out_shape=shapes,
+        in_specs=[VM] * 5,
+        out_specs=[VM] * 5,
+        name="handed_on",
+    )(output, dq, kg, vg, weight)
     return output, dq, kg, vg, weight.reshape(256, 512)
 
 

time: 76 us -> 70.4 us (0.926)
  the two profiles are of different devices: /device:TPU:16 before, /device:TPU:1 now
where the time goes in v3:
time: 70.4 us; the launch traced here: 69.5 us
  Pallas kernels  68.9 us (98%)
    pallas_call x1, Pallas kernels, on_device(): pl.pallas_call(layer_kernel, out_shape=[T, T, T, T, jax.ShapeDtypeStruct(...  66.4 us
    pallas_call x1, Pallas kernels, on_device(): pl.pallas_call(handed_on, out_shape=shapes, in_specs=[VM] * 5, out_specs=...  2.52 us

profile of v3, /device:TPU:1, one launch (start us, length us, event | category | flops | bytes accessed | tf_op | source)
XLA Modules:
  0.0 69.5 jit_solution(9345508348693214999)
XLA Ops:
  0.6 66.4 %layer.1 = (bf16[512,256]{1,0:T(8,128)(2,1)}, bf16[512,256]{1,0:T(8,128)(2,1)}, bf16[512,256]{1,0:T(8,128)(2,1)}, bf16[512,256]{1,0:T(8,128)(2,1)}, f32[2,4,32,512]{3,2,1,0:T(8,128)}) custom-call(bf16[512,256]{1,0:T(8,128)(2,1)} %q_hbm.1, bf16[512,256]{1,0:T(8,128)(2,1)} %k_hbm.1, bf16[512,256]{1,0:T(8,128)(2,1)} %v_hbm.1, bf16[512,256]{1,0:T(8,128)(2,1)} %g_hbm.1, ...), custom_call_target="tpu_custom_call" | custom-call | tf_op jit(solution)/shard_map/layer/pallas_call | solution.py:528
  67.0 2.5 %handed_on.1 = (bf16[512,256]{1,0:T(8,128)(2,1)}, bf16[512,256]{1,0:T(8,128)(2,1)}, bf16[512,256]{1,0:T(8,128)(2,1)}, bf16[512,256]{1,0:T(8,128)(2,1)}, f32[2,4,32,512]{3,2,1,0:T(8,128)}) custom-call(bf16[512,256]{1,0:T(8,128)(2,1)} %get-tuple-element.15.refs_0_, bf16[512,256]{1,0:T(8,128)(2,1)} %get-tuple-element.16.refs_1_, ...), custom_call_target="tpu_custom_call" | custom-call | tf_op jit(solution)/shard_map/handed_on/pallas_call | solution.py:551

commit v4 on v3

--- a/solution.py
+++ b/solution.py
@@ -65,7 +65,6 @@
         peers = [self.core, self.far, self.head, *[self.next_plane(d) for d in (1, 2, 3, -1, -2, -3)], self.next_shard(1), self.next_shard(-1)]
         peers += [{"z": self.along_z(i)} for i in range(1, 8)]
         peers += [{"x": self.along_x(i)} for i in range(1, 4)]
-        peers += [{"x": self.along_x(i), "yh": 1 - self.yh} for i in range(1, 4)]
         if diagonal:
             peers.append(self.diagonal)
         barrier = pltpu.get_barrier_semaphore()
@@ -95,7 +94,7 @@
 
 def layer_kernel(q_hbm, k_hbm, v_hbm, g_hbm, w_hbm, keep_ref, frame_ref,
                  out_hbm, dq_hbm, kg_hbm, vg_hbm, weight_hbm,
-                 out_ref, dq_ref, kg_ref, vg_ref, weight_ref,
+                 out_ref, dq_ref, kg_ref, vg_ref,
                  q, k, v, g, w, rim, go, wo, pooled, win, last, coarse, coarse4, mixed,
                  kaug, vcat, kt, vt, qaugT, gT, qm, gm, sbuf, dbuf, pbuf, tops, stats,
                  attT, att, atto, dqT, wg, wgb, wgr, wx, wxr, wz, wzr, wall,
@@ -470,10 +469,6 @@
     to_line = [mail.send(line, line, {"x": at.along_x(i)}) for i in range(1, 4)]
     to_far1.wait_recv()
     to_own1 = to_owners(1)
-    to_att.wait_recv()
-    to_wo.wait_recv()
-    out_ref[...] = (dot(att[...], w[:, lanes(h)]) + dot(atto[...], wo[...])).astype(BF16)
-    store(1, out_ref, out_hbm)
     for copy in to_cz:
         copy.wait_recv()
     total = up(cz[:, z])
@@ -481,6 +476,10 @@
         total = total + up(czr[i])
     cp[...] = total.astype(BF16)
     to_cp = [mail.send(cp, cpr.at[n], who) for n, who in enumerate((at.far, at.core, at.diagonal))]
+    to_att.wait_recv()
+    to_wo.wait_recv()
+    out_ref[...] = (dot(att[...], w[:, lanes(h)]) + dot(atto[...], wo[...])).astype(BF16)
+    store(1, out_ref, out_hbm)
     for copy in to_line:
         copy.wait_recv()
     to_half = mail.send(lines.at[c], lines.at[c], at.core)
@@ -490,8 +489,7 @@
         cfull[r, :, lanes(c, 128)] = up(cp[r]) + up(cpr[0, r])
         cfull[r, :, lanes(1 - c, 128)] = up(cpr[1, r]) + up(cpr[2, r])
     to_half.wait_recv()
-    weight_ref[...] = up(lines[...])
-    store(4, weight_ref, weight_hbm)
+    store(4, lines, weight_hbm)
     token = lax.broadcasted_iota(jnp.int32, (512, 80), 0)
     row = lax.broadcasted_iota(jnp.int32, (512, 80), 1)
     spread = jnp.where(jnp.where(row < 64, token // MIDG, 64 + 4 * shard + token // FARG) == row, 1.0, 0.0).astype(BF16)
@@ -518,8 +516,9 @@
 
 
 def handed_on(*refs):
-    for n in range(5):
+    for n in range(4):
         refs[5 + n][...] = refs[n][...]
+    refs[9][...] = up(refs[4][...])
 
 
 def on_device(queries, key_vectors, value_vectors, out_grad, out_weight, mid_keep, frame_keep):
@@ -527,11 +526,11 @@
     T = jax.ShapeDtypeStruct((512, 256), BF16)
     output, dq, kg, vg, weight = pl.pallas_call(
         layer_kernel,
-        out_shape=[T, T, T, T, jax.ShapeDtypeStruct((2, 4, 32, 512), F32)],
+        out_shape=[T, T, T, T, jax.ShapeDtypeStruct((2, 4, 32, 512), BF16)],
         in_specs=[ANY] * 5 + [SM] * 2,
         out_specs=[ANY] * 5,
         scratch_shapes=[
-            B(512, 256), B(512, 256), B(512, 256), B(512, 256), S(2, 4, 32, 512),
+            B(512, 256), B(512, 256), B(512, 256), B(512, 256),
             B(512, 256), B(512, 256), B(512, 256), B(512, 256), B(256, 512), B(256, 512), B(512, 256), B(256, 256),
             B(4, 64, 512), B(3, 4, 64, 512), B(4, 64, 512), B(32, 16, 512), B(4, 16, 512), B(512, 256),
             B(2, 8, 256, 256), B(2, 8, 256, 128), B(2, 8, 128, 256), B(2, 8, 128, 256),

time: 70.4 us -> 69.4 us (0.986); the launches traced: 69.5 us -> 69.3 us
  no operation moved by 1% of the time
where the time goes in v4:
time: 69.4 us; the launch traced here: 69.3 us
  Pallas kernels  68.6 us (99%)
    pallas_call x1, Pallas kernels, on_device(): pl.pallas_call(layer_kernel, out_shape=[T, T, T, T, jax.ShapeDtypeStruct(...  66.2 us
    pallas_call x1, Pallas kernels, on_device(): pl.pallas_call(handed_on, out_shape=shapes, in_specs=[VM] * 5, out_specs=...  2.43 us

profile of v4, /device:TPU:1, one launch (start us, length us, event | category | flops | bytes accessed | tf_op | source)
XLA Modules:
  0.0 69.3 jit_solution(5585923899261155142)
XLA Ops:
  0.6 66.2 %layer.1 = (bf16[512,256]{1,0:T(8,128)(2,1)}, bf16[512,256]{1,0:T(8,128)(2,1)}, bf16[512,256]{1,0:T(8,128)(2,1)}, bf16[512,256]{1,0:T(8,128)(2,1)}, bf16[2,4,32,512]{3,2,1,0:T(8,128)(2,1)}) custom-call(bf16[512,256]{1,0:T(8,128)(2,1)} %q_hbm.1, bf16[512,256]{1,0:T(8,128)(2,1)} %k_hbm.1, bf16[512,256]{1,0:T(8,128)(2,1)} %v_hbm.1, bf16[512,256]{1,0:T(8,128)(2,1)} %g_hbm.1, ...), custom_call_target="tpu_custom_call" | custom-call | tf_op jit(solution)/shard_map/layer/pallas_call | solution.py:527
  66.9 2.4 %handed_on.1 = (bf16[512,256]{1,0:T(8,128)(2,1)}, bf16[512,256]{1,0:T(8,128)(2,1)}, bf16[512,256]{1,0:T(8,128)(2,1)}, bf16[512,256]{1,0:T(8,128)(2,1)}, f32[2,4,32,512]{3,2,1,0:T(8,128)}) custom-call(bf16[512,256]{1,0:T(8,128)(2,1)} %get-tuple-element.15.refs_0_, bf16[512,256]{1,0:T(8,128)(2,1)} %get-tuple-element.16.refs_1_, ...), custom_call_target="tpu_custom_call" | custom-call | tf_op jit(solution)/shard_map/handed_on/pallas_call | solution.py:550

commit v5 on v4

--- a/solution.py
+++ b/solution.py
@@ -296,12 +296,6 @@
         copy.wait_recv()
     whole = coarse.at[:, :, half]
     share_coarse = mail.send(whole, whole, at.core)
-    loads[3].wait()
-    to_g.wait_recv()
-    mixed[...] = (dot_nt(g[...], w[:, lanes(h)]) + dot_nt(go[...], w[:, lanes(1 - h)])).astype(BF16)
-    for b in range(2):
-        for r in range(2):
-            by_head(mixed, b, r, gT, gm)
     share_a3.wait_recv()
     share_b3.wait_recv()
     beside_a.wait_recv()
@@ -313,6 +307,9 @@
     score(6)
     score(7)
 
+    loads[3].wait()
+    to_wo = mail.send(w.at[:, lanes(1 - h)], wo, at.head)
+    to_att = []
     for r in range(2):
         for b in range(2):
             top = jnp.max(tops[b, r], axis=0, keepdims=True)
@@ -332,14 +329,19 @@
                     mix[head] = mix[head] + dot(vt[r, ci, 64 * head:64 * head + 64, :], pr[:, 256 * head:256 * head + 256])
             for head in range(2):
                 attT[r, 64 * head:64 * head + 64, 256 * b:256 * b + 256] = mix[head].astype(BF16)
-        att[:, 128 * r:128 * r + 128] = attT[r].T
+        part = slice(128 * r, 128 * r + 128)
+        att[:, part] = attT[r].T
+        to_att.append(mail.send(att.at[:, part], atto.at[:, part], at.head))
+    to_g.wait_recv()
     turned = attT[...].reshape(256, 512)
     wg[:, lanes(h)] = dot(turned, g[...]) * (1.0 / 256.0)
     wg[:, lanes(1 - h)] = dot(turned, go[...]) * (1.0 / 256.0)
     wgb[...] = wg[pl.ds(pl.multiple_of(128 * (1 - c), 128), 128), :].astype(BF16)
     to_w = mail.send(wgb, wgr, at.core)
-    to_att = mail.send(att, atto, at.head)
-    to_wo = mail.send(w.at[:, lanes(1 - h)], wo, at.head)
+    mixed[...] = (dot_nt(g[...], w[:, lanes(h)]) + dot_nt(go[...], w[:, lanes(1 - h)])).astype(BF16)
+    for b in range(2):
+        for r in range(2):
+            by_head(mixed, b, r, gT, gm)
     for b in range(2):
         for r in range(2):
             dqT[b, r] = jnp.zeros((128, 256), F32)
@@ -476,7 +478,8 @@
         total = total + up(czr[i])
     cp[...] = total.astype(BF16)
     to_cp = [mail.send(cp, cpr.at[n], who) for n, who in enumerate((at.far, at.core, at.diagonal))]
-    to_att.wait_recv()
+    for copy in to_att:
+        copy.wait_recv()
     to_wo.wait_recv()
     out_ref[...] = (dot(att[...], w[:, lanes(h)]) + dot(atto[...], wo[...])).astype(BF16)
     store(1, out_ref, out_hbm)
@@ -542,7 +545,7 @@
             S(2, 2, 4, 64, 256), B(2, 4, 64, 256), B(2, 4, 64, 256), B(2, 3, 64, 256), B(2, 3, 64, 256), B(2, 4, 32, 512),
             B(2, 32, 16, 256), B(2, 32, 16, 128), B(2, 32, 16, 128), B(3, 2, 8, 16, 128), B(2, 8, 16, 128),
             B(7, 2, 16, 128), B(2, 16, 128), B(3, 2, 16, 128), S(2, 16, 256),
-            pltpu.SemaphoreType.DMA((5,)), pltpu.SemaphoreType.DMA((5,)), pltpu.SemaphoreType.DMA((90,)), pltpu.SemaphoreType.DMA((90,))],
+            pltpu.SemaphoreType.DMA((5,)), pltpu.SemaphoreType.DMA((5,)), pltpu.SemaphoreType.DMA((91,)), pltpu.SemaphoreType.DMA((91,))],
         compiler_params=pltpu.CompilerParams(collective_id=0, has_side_effects=True, vmem_limit_bytes=60 * 2**20),
         name="layer",
     )(queries, key_vectors, value_vectors, out_grad, out_weight, mid_keep, frame_keep)

time: 69.4 us -> 69.7 us (level)
  no operation moved by 1% of the time
where the time goes in v5:
time: 69.7 us; the launch traced here: 68.9 us
  Pallas kernels  68.3 us (98%)
    pallas_call x1, Pallas kernels, on_device(): pl.pallas_call(layer_kernel, out_shape=[T, T, T, T, jax.ShapeDtypeStruct(...  65.9 us
    pallas_call x1, Pallas kernels, on_device(): pl.pallas_call(handed_on, out_shape=shapes, in_specs=[VM] * 5, out_specs=...  2.43 us

profile of v5, /device:TPU:1, one launch (start us, length us, event | category | flops | bytes accessed | tf_op | source)
XLA Modules:
  0.0 68.9 jit_solution(1388413096262708568)
XLA Ops:
  0.6 65.9 %layer.1 = (bf16[512,256]{1,0:T(8,128)(2,1)}, bf16[512,256]{1,0:T(8,128)(2,1)}, bf16[512,256]{1,0:T(8,128)(2,1)}, bf16[512,256]{1,0:T(8,128)(2,1)}, bf16[2,4,32,512]{3,2,1,0:T(8,128)(2,1)}) custom-call(bf16[512,256]{1,0:T(8,128)(2,1)} %q_hbm.1, bf16[512,256]{1,0:T(8,128)(2,1)} %k_hbm.1, bf16[512,256]{1,0:T(8,128)(2,1)} %v_hbm.1, bf16[512,256]{1,0:T(8,128)(2,1)} %g_hbm.1, ...), custom_call_target="tpu_custom_call" | custom-call | tf_op jit(solution)/shard_map/layer/pallas_call | solution.py:530
  66.5 2.4 %handed_on.1 = (bf16[512,256]{1,0:T(8,128)(2,1)}, bf16[512,256]{1,0:T(8,128)(2,1)}, bf16[512,256]{1,0:T(8,128)(2,1)}, bf16[512,256]{1,0:T(8,128)(2,1)}, f32[2,4,32,512]{3,2,1,0:T(8,128)}) custom-call(bf16[512,256]{1,0:T(8,128)(2,1)} %get-tuple-element.15.refs_0_, bf16[512,256]{1,0:T(8,128)(2,1)} %get-tuple-element.16.refs_1_, ...), custom_call_target="tpu_custom_call" | custom-call | tf_op jit(solution)/shard_map/handed_on/pallas_call | solution.py:553
